TPU v7x, 128 devices: a whole 4x4x4 slice. The times are simulated.
128 devices in a mesh: ctx: 8 (over y, z_hi), fsdp: 16 (over z_lo, x, core).
Axes of the slice: x: 4, y: 4, z: 4 (z_hi: 2, z_lo: 2; z = z_hi * 2 + z_lo), core: 2. Of those that a mesh axis runs over, the one named last changes fastest.
Arguments:
- tokens: bfloat16 [16, 1024, 2048], P('fsdp', 'ctx'), may hold values from -6 to 6
- cotangent: bfloat16 [16, 1024, 2048], P('fsdp', 'ctx'), may hold values from -6 to 6
- w_qkv: bfloat16 [2048, 6144], P(('ctx', 'fsdp')), may hold values from -0.125 to 0.125
- w_out: bfloat16 [2048, 2048], P(('ctx', 'fsdp')), may hold values from -0.5 to 0.5
- w_router: bfloat16 [2048, 16], P(('ctx', 'fsdp')), may hold values from -0.0625 to 0.0625
- norm_attn: bfloat16 [2048], P(('ctx', 'fsdp')), may hold values from 0.099609375 to 1.8984375
- norm_moe: bfloat16 [2048], P(('ctx', 'fsdp')), may hold values from 0.099609375 to 1.8984375
- query_gain: bfloat16 [2048], P(('ctx', 'fsdp')), may hold values from 0.796875 to 2
- key_gain: bfloat16 [2048], P(('ctx', 'fsdp')), may hold values from 0.796875 to 2
- w_gate_up: bfloat16 [16, 2048, 2048], P('ctx', 'fsdp'), may hold values from -0.125 to 0.125
- w_down: bfloat16 [16, 1024, 2048], P('ctx', None, 'fsdp'), may hold values from -0.5 to 0.5
- routes: int32 [16, 1024, 4], P('fsdp'), may hold values from 0 to 15, all different within a row; in each aligned block of 1024 rows (0 to 1023, 1024 to 2047, ..., all dimensions but the last counted through in order) at most 384 rows name the same one
- block_order: int32 [16, 8], P('fsdp', 'ctx'), may hold values from 0 to 7, each once within a row
Outputs:
- layer_output: bfloat16 [16, 1024, 2048], P('fsdp', 'ctx')
- grad_tokens: bfloat16 [16, 1024, 2048], P('fsdp', 'ctx')
- grad_w_qkv: float32 [2048, 6144], P(('ctx', 'fsdp'))
- grad_w_out: float32 [2048, 2048], P(('ctx', 'fsdp'))
- grad_w_router: float32 [2048, 16], P(('ctx', 'fsdp'))
- grad_norm_attn: float32 [2048], P(('ctx', 'fsdp'))
- grad_norm_moe: float32 [2048], P(('ctx', 'fsdp'))
- grad_query_gain: float32 [2048], P(('ctx', 'fsdp'))
- grad_key_gain: float32 [2048], P(('ctx', 'fsdp'))
- grad_w_gate_up: float32 [16, 2048, 2048], P('ctx', 'fsdp')
- grad_w_down: float32 [16, 1024, 2048], P('ctx', None, 'fsdp')
Inputs may be any that keep to these rules, and one draw needn't show every extreme that they name: `routes`: each row names 4 different experts. In each sequence no expert is named by more than 384 rows, and some sequence has an expert named by exactly 384. `block_order`: each sequence's row is a permutation of the block numbers.
All inputs are finite; a program needn't handle non-finite values.
Results may differ from a plain program's by a relative error of at most 0.028.
Values may be sent and summed in bfloat16 or wider, within the bound.
No kernel may reach another device: no remote copies, remote signals or barrier semaphores. Data moves between devices by JAX's collectives and lax.ppermute only.
A program may use at most 384 MiB of HBM per device.

v0:
```python
import jax
import jax.numpy as jnp
import numpy as np
from jax import lax
from jax.sharding import Mesh, PartitionSpec as P

D = 2048
HALF = 1024
HEAD_DIM = 128
FF = 1024
CAP = 384
ROWS = 128
SCALE = HEAD_DIM**-0.5

epsilon = 1e-06
rope_base = 10000.0


def f32(a):
    return a.astype(jnp.float32)


def bf16(a):
    return a.astype(jnp.bfloat16)


def dot(a, b):
    return jnp.dot(a, b, preferred_element_type=jnp.float32)


def dot_t(a, b):
    return lax.dot_general(a, b, (((1,), (1,)), ((), ())), preferred_element_type=jnp.float32)


def t_dot(a, b):
    return lax.dot_general(a, b, (((0,), (0,)), ((), ())), preferred_element_type=jnp.float32)


def other_core(a):
    return lax.ppermute(a, "c", [(0, 1), (1, 0)])


def from_chip(a, step):
    return lax.ppermute(a, "y", [(i, (i + step) % 4) for i in range(4)])


def y_gather(a):
    return [a] + [from_chip(a, step) for step in (1, 2, 3)]


def y_scatter(parts):
    return [parts[0]] + [from_chip(parts[step], 4 - step) for step in (1, 2, 3)]


def by_distance(a, y):
    place = (y - jnp.arange(4)) % 4
    hit = place[:, None] == jnp.arange(4)[None, :]
    return jnp.sum(jnp.where(hit[None, :, :, None], a[:, None], jnp.zeros((), a.dtype)), axis=2)


def chosen(a, place):
    hit = place[:, None] == jnp.arange(4)[None, :]
    hit = hit.reshape(4, 4, *[1] * (a.ndim - 1))
    return jnp.sum(jnp.where(hit, a[None], jnp.zeros((), a.dtype)), axis=1)


def trade(pieces, y, c):
    pairs = pieces.reshape(4, 2, *pieces.shape[1:])
    mine = jnp.where(c == 0, pairs[:, 0], pairs[:, 1])
    theirs = jnp.where(c == 0, pairs[:, 1], pairs[:, 0])
    got = other_core(theirs)
    both = jnp.where(c == 0, jnp.stack([mine, got], 1), jnp.stack([got, mine], 1))
    both = chosen(both, (y + jnp.arange(4)) % 4)
    got = jnp.stack([both[0]] + [from_chip(both[step], step) for step in (1, 2, 3)])
    return chosen(got, (y - jnp.arange(4)) % 4).reshape(pieces.shape)


def ring_sum(a, y):
    n = a.shape[0]
    a = a + other_core(a)
    a = by_distance(a.reshape(n, 4, 256), y)
    a = a + from_chip(a, 1) + from_chip(a, 2) + from_chip(a, 3)
    return by_distance(a, y).reshape(n, 1024)


def angle_tables():
    frequency = rope_base ** (-2.0 * np.arange(64) / HEAD_DIM)
    blocks = np.arange(8)[:, None] * ROWS * frequency[None]
    rows = np.arange(ROWS)[:, None] * frequency[None]
    tables = (np.cos(blocks), np.sin(blocks), np.cos(rows), np.sin(rows))
    return [jnp.asarray(table, jnp.float32) for table in tables]


def split_halves(a):
    blocks = [a[..., k * 128 : k * 128 + 128] for k in range(a.shape[-1] // 128)]
    return jnp.concatenate(blocks[0::2], axis=-1), jnp.concatenate(blocks[1::2], axis=-1)


def join_halves(low, high):
    blocks = []
    for k in range(low.shape[-1] // 128):
        blocks += [low[..., k * 128 : k * 128 + 128], high[..., k * 128 : k * 128 + 128]]
    return jnp.concatenate(blocks, axis=-1)


def other_layer(a):
    return lax.ppermute(a, "zh", [(0, 1), (1, 0)])


def to_half(low, high, zh, c):
    mine = jnp.where(c == 0, low, high)
    got = other_core(jnp.where(c == 0, high, low))
    keep = jnp.where(zh == c, mine, got)
    got = other_layer(jnp.where(zh == c, got, mine))
    return jnp.where(zh == 0, keep, got), jnp.where(zh == 0, got, keep)


def from_half(a, zh, c):
    first, second = a[:ROWS], a[ROWS:]
    mine = jnp.where(zh == 0, first, second)
    got = other_layer(jnp.where(zh == 0, second, first))
    keep = jnp.where(zh == c, mine, got)
    got = other_core(jnp.where(zh == c, got, mine))
    return join_halves(jnp.where(c == 0, keep, got), jnp.where(c == 0, got, keep))


def turn(values, cosine, sine):
    out = []
    for at in (0, 128):
        first, second = values[:, at : at + 64], values[:, at + 64 : at + 128]
        out += [first * cosine - second * sine, second * cosine + first * sine]
    return jnp.concatenate(out, axis=1)


def heads_of(a):
    return a.reshape(1024, 2, 128)


def attend(query, key, value):
    scores = jnp.einsum(
        "thd,shd->hts", heads_of(query), heads_of(key), preferred_element_type=jnp.float32
    )
    scores = scores * SCALE
    weights = jnp.exp(scores - jnp.max(scores, axis=-1, keepdims=True))
    probs = weights / jnp.sum(weights, axis=-1, keepdims=True)
    attended = jnp.einsum(
        "hts,shd->thd", bf16(probs), heads_of(value), preferred_element_type=jnp.float32
    )
    return bf16(attended.reshape(1024, 256)), probs


def attend_back(d_att, query, key, value, probs):
    d_att, query, key, value = (heads_of(a) for a in (d_att, query, key, value))
    d_probs = jnp.einsum("thd,shd->hts", d_att, value, preferred_element_type=jnp.float32)
    d_scores = bf16(probs * (d_probs - jnp.sum(probs * d_probs, axis=-1, keepdims=True)))
    d_value = jnp.einsum("hts,thd->shd", bf16(probs), d_att, preferred_element_type=jnp.float32)
    d_key = jnp.einsum("hts,thd->shd", d_scores, query, preferred_element_type=jnp.float32)
    d_query = jnp.einsum("hts,shd->thd", d_scores, key, preferred_element_type=jnp.float32)
    return tuple(a.reshape(1024, 256) for a in (d_query * SCALE, d_key * SCALE, d_value))


def per_expert(pattern, a, b):
    return jnp.einsum(pattern, a, b, preferred_element_type=jnp.float32)


def open_experts(seat, gate, normed, cot, weights):
    taken = jnp.arange(CAP, dtype=jnp.int32)[None, :, None] == seat
    pick = taken.astype(jnp.bfloat16)
    weight = jnp.sum(jnp.where(taken, gate, 0.0), axis=2)[:, :, None]
    rows = bf16(per_expert("hst,td->hsd", pick, normed))
    cot_rows = per_expert("hst,td->hsd", pick, cot)
    d_out = bf16(weight * cot_rows)
    part = jnp.concatenate(
        [
            bf16(per_expert("hsd,hdf->hsf", rows, weights[:, :, : 2 * FF])),
            bf16(per_expert("hsd,hdf->hsf", d_out, weights[:, :, 2 * FF :])),
        ],
        axis=2,
    )
    return part, rows, d_out, bf16(cot_rows), pick, taken, weight


def close_experts(own, received, state, weights, before):
    rows, d_out, cot_rows, pick, taken, weight = state
    part = f32(own) + f32(received)
    gate, up, d_hidden = part[:, :, :FF], part[:, :, FF : 2 * FF], part[:, :, 2 * FF :]
    sig = jax.nn.sigmoid(gate)
    hidden = bf16(gate * sig * up)
    out = per_expert("hsf,hdf->hsd", hidden, weights[:, :, 2 * FF :])
    d_weight = jnp.sum(out * f32(cot_rows), axis=2)
    d_token = jnp.sum(jnp.where(taken, d_weight[:, :, None], 0.0), axis=1)
    d_gate = bf16(d_hidden * up * sig * (1.0 + gate * (1.0 - sig)))
    d_gate_up = jnp.concatenate([d_gate, bf16(d_hidden * gate * sig)], axis=2)
    d_rows = bf16(per_expert("hsf,hdf->hsd", d_gate_up, weights[:, :, : 2 * FF]))
    both = jnp.concatenate([bf16(weight * out), d_rows], axis=2)
    pick, both = pick.reshape(2 * CAP, 1024), both.reshape(2 * CAP, 2 * HALF)
    found = t_dot(pick, both)
    if before is not None:
        found = found + before
    return found, (rows, d_out, d_gate_up, hidden), d_token


def expert_products(rows, d_out, d_gate_up, hidden):
    left = jnp.concatenate([rows, d_out], axis=1)
    right = jnp.concatenate(
        [
            jnp.pad(d_gate_up, ((0, 0), (0, 0), (0, FF))),
            jnp.pad(hidden, ((0, 0), (0, 0), (2 * FF, 0))),
        ],
        axis=1,
    )
    return bf16(per_expert("hsd,hsf->hdf", left, right)).reshape(D, 3 * FF)


def on_device(
    tokens,
    cotangent,
    w_qkv,
    w_out,
    w_router,
    norm_attn,
    norm_moe,
    query_gain,
    key_gain,
    w_gate_up,
    w_down,
    routes,
    block_order,
):
    y, zh, c = lax.axis_index("y"), lax.axis_index("zh"), lax.axis_index("c")
    plane = ("zh", "zl", "x")
    own_first = c == 0

    low, high = split_halves(tokens[0])
    low, high, w_qkv = lax.optimization_barrier((low, high, w_qkv))
    x_blocks = jnp.concatenate(to_half(low, high, zh, c))
    x_blocks, block_order, w_gate_up, cotangent, routes = lax.optimization_barrier(
        (x_blocks, block_order, w_gate_up, cotangent, routes)
    )
    x_own = y_gather(x_blocks)
    x_par = [other_core(part) for part in x_own]
    place = jnp.full((8, 128), block_order[0, 0], jnp.int32).astype(jnp.float32)
    places = y_gather(jnp.stack(to_half(place, place, zh, c)))
    places = jnp.stack(places)[:, :, 0, 0].reshape(8)

    pieces = w_qkv.reshape(16, 3, 8, 256).transpose(2, 0, 1, 3).reshape(8, 16, 768)
    small = jnp.concatenate(
        [norm_attn[:, None], norm_moe[:, None], w_router, query_gain[:, None], key_gain[:, None]],
        axis=1,
    )
    small = jnp.pad(small, ((0, 0), (0, 108)))
    pieces = jnp.concatenate([pieces, jnp.broadcast_to(small, (8, 16, 128))], axis=2)
    pieces = trade(pieces, y, c).reshape(128, 896)
    out_low, out_high = split_halves(w_out)
    out_par = other_core(jnp.where(own_first, out_high, out_low))
    out_own = jnp.where(own_first, out_low, out_high)
    out_both = jnp.where(
        own_first, jnp.concatenate([out_own, out_par]), jnp.concatenate([out_par, out_own])
    )
    out_both = out_both.reshape(32, 4, 256).transpose(1, 0, 2).reshape(128, 256)
    dense = jnp.concatenate([pieces, out_both], axis=1)
    dense, w_gate_up = lax.optimization_barrier((dense, w_gate_up))
    dense = lax.all_gather(dense, plane, axis=0, tiled=True).reshape(2, 2, 4, 4, 2, 16, 1152)

    down_t = w_down.transpose(0, 2, 1)
    expert_w = [
        lax.all_gather(
            jnp.concatenate([w_gate_up[m], down_t[m]], axis=1), plane, axis=0, tiled=True
        ).reshape(2, HALF, 3 * FF)
        for m in range(2)
    ]

    cot_low, cot_high = split_halves(cotangent[0])
    cot_here = jnp.concatenate(to_half(cot_low, cot_high, zh, c))
    cot_sent, x_own = lax.optimization_barrier((cot_here, x_own))
    cot_parts = y_gather(cot_sent)
    route_t = routes[0].T
    route_t = jnp.where(c == zh, route_t, other_core(route_t))
    route_t = by_distance(route_t.reshape(4, 4, 256), y).reshape(4, 1024)

    def rolled(a):
        a = a.transpose(1, 3, 0, 2, 4, 5, 6).reshape(2, HALF, -1)
        return jnp.where(own_first, a, a[::-1])

    qkv_w = rolled(dense[..., :768]).reshape(D, 768)
    small_all = dense[..., 768:788]
    small_rolled = f32(rolled(small_all))
    gain_attn = small_rolled[:, :, 0]
    gain_moe = small_rolled[0, :, 1]
    router_w = bf16(small_rolled[0, :, 2:18])
    small_true = f32(small_all[..., 18:20].transpose(3, 0, 1, 2, 4, 5, 6).reshape(8, 256, 2))
    head_block = y * 2 + c
    mine = lax.dynamic_index_in_dim(small_true, head_block, 0, keepdims=False)
    gain_query, gain_key = mine[:, 0], mine[:, 1]
    out_w = dense.reshape(16, 128, 1152)[:, :, 896:].reshape(16, 4, 32, 256)
    out_w = out_w.transpose(0, 2, 1, 3).reshape(2, 256, HALF)
    out_w = jnp.where(own_first, out_w, out_w[::-1]).reshape(512, HALF)

    x_own_all, x_par_all = f32(jnp.concatenate(x_own)), f32(jnp.concatenate(x_par))
    square = jnp.sum(x_own_all * x_own_all, axis=1) + jnp.sum(x_par_all * x_par_all, axis=1)
    rstd_one = lax.rsqrt(square / D + epsilon)[:, None]
    normed_one = jnp.concatenate(
        [bf16(x_own_all * rstd_one * gain_attn[0]), bf16(x_par_all * rstd_one * gain_attn[1])],
        axis=1,
    )
    qkv = dot(normed_one, qkv_w)
    squares = jnp.stack(
        [
            jnp.sum(qkv[:, :256] * qkv[:, :256], axis=1),
            jnp.sum(qkv[:, 256:512] * qkv[:, 256:512], axis=1),
        ]
    )
    rstd = lax.rsqrt(ring_sum(squares, y) / D + epsilon)
    rstd_q, rstd_k = rstd[0][:, None], rstd[1][:, None]
    here = places[:, None, None] == jnp.arange(8, dtype=jnp.float32)[None, :, None]
    block_cos, block_sin, row_cos, row_sin = angle_tables()
    block_cos = jnp.sum(jnp.where(here, block_cos, 0.0), axis=1)[:, None]
    block_sin = jnp.sum(jnp.where(here, block_sin, 0.0), axis=1)[:, None]
    cosine = block_cos * row_cos - block_sin * row_sin
    sine = block_sin * row_cos + block_cos * row_sin
    cosine, sine = cosine.reshape(1024, 64), sine.reshape(1024, 64)
    qkv, out_w, cosine, sine = lax.optimization_barrier((qkv, out_w, cosine, sine))
    query_hat, key_hat = qkv[:, :256] * rstd_q, qkv[:, 256:512] * rstd_k
    heads = (
        bf16(turn(query_hat * gain_query, cosine, sine)),
        bf16(turn(key_hat * gain_key, cosine, sine)),
        bf16(qkv[:, 512:]),
    )
    attended, probs = attend(*heads)
    attended, cot_parts = lax.optimization_barrier((attended, cot_parts))
    cot_all = jnp.concatenate(cot_parts)
    attended = jnp.concatenate([attended, other_core(attended)], axis=1)
    out_part = dot(attended, out_w).reshape(4, 256, HALF)
    got = y_scatter([out_part[0]] + [bf16(out_part[s]) for s in (1, 2, 3)])
    x_here = f32(x_own[0])
    after = x_here + sum(f32(g) for g in got)

    square = jnp.sum(after * after, axis=1)
    rstd_two = lax.rsqrt((square + other_core(square)) / D + epsilon)[:, None]
    after_hat = after * rstd_two
    normed_two = bf16(after_hat * gain_moe)
    normed_all = jnp.concatenate(y_gather(normed_two))
    logits = lax.dot_general(
        router_w, normed_all, (((0,), (1,)), ((), ())), preferred_element_type=jnp.float32
    )
    logits = logits + other_core(logits)
    picked = route_t[:, None, :] == jnp.arange(16, dtype=jnp.int32)[None, :, None]
    gates = jax.nn.softmax(jnp.sum(jnp.where(picked, logits[None], 0.0), axis=1), axis=0)

    found, d_gates, saved = None, jnp.zeros((4, 1024), jnp.float32), []
    for m in range(2):
        chosen_here = route_t[None] == y * 4 + jnp.arange(2, dtype=jnp.int32)[:, None, None] * 2 + m
        hit = jnp.sum(chosen_here.astype(jnp.int32), axis=1)
        rank = jnp.cumsum(hit, axis=1) - hit
        seat = jnp.where(hit > 0, rank, CAP)[:, None]
        gate_token = jnp.sum(jnp.where(chosen_here, gates[None], 0.0), axis=1)[:, None]
        part, *state = open_experts(seat, gate_token, normed_all, cot_all, expert_w[m])
        found, kept, d_token = close_experts(part, other_core(part), state, expert_w[m], found)
        saved.append(kept)
        d_gates = d_gates + jnp.sum(jnp.where(chosen_here, d_token[:, None], 0.0), axis=0)
    first_grads = expert_products(*saved[0])
    found, first_grads = lax.optimization_barrier((found, first_grads))
    expert_grads = [lax.psum_scatter(first_grads, plane, scatter_dimension=0, tiled=True)]
    moe_sum, d_normed = bf16(found[:, :HALF]), bf16(found[:, HALF:])

    def ring_scatter(a):
        a = a.reshape(4, 256, HALF)
        return sum(f32(g) for g in y_scatter([a[s] for s in range(4)]))

    d_normed_here = ring_scatter(d_normed)
    d_normed_here, kept = lax.optimization_barrier((d_normed_here, saved[1]))
    second_grads = expert_products(*kept)
    d_gates = d_gates.reshape(4, 4, 256)
    d_gates = sum(y_scatter([d_gates[:, s] for s in range(4)]))
    d_gates = d_gates + other_core(d_gates)

    gates_here, picked_here = gates[:, :256], picked[:, :, :256]
    d_routed = gates_here * (d_gates - jnp.sum(gates_here * d_gates, axis=0, keepdims=True))
    d_logits = jnp.sum(jnp.where(picked_here, d_routed[:, None, :], 0.0), axis=0)
    grad_router = lax.dot_general(
        f32(normed_two), d_logits, (((0,), (1,)), ((), ())), preferred_element_type=jnp.float32
    )
    d_through = lax.dot_general(
        d_logits, f32(router_w), (((0,), (1,)), ((), ())), preferred_element_type=jnp.float32
    )
    d_normed_here = d_normed_here + d_through
    grad_norm_moe = jnp.sum(d_normed_here * after_hat, axis=0)
    d_scaled = d_normed_here * gain_moe
    along = jnp.sum(d_scaled * after_hat, axis=1)
    along = (along + other_core(along))[:, None] / D
    d_after = f32(cot_here) + rstd_two * (d_scaled - after_hat * along)

    d_attn = jnp.concatenate(y_gather(bf16(d_after)))
    moe_sum, d_attn = lax.optimization_barrier((moe_sum, d_attn))
    moe_here = ring_scatter(moe_sum)
    d_att = dot_t(d_attn, out_w)
    d_att = bf16(d_att[:, :256] + other_core(d_att[:, 256:]))
    d_att, expert_grads[0], second_grads = lax.optimization_barrier(
        (d_att, expert_grads[0], second_grads)
    )
    expert_grads.append(lax.psum_scatter(second_grads, plane, scatter_dimension=0, tiled=True))
    d_query, d_key, d_value = attend_back(d_att, *heads, probs)
    d_query, d_key = turn(d_query, cosine, -sine), turn(d_key, cosine, -sine)
    d_query, d_attn = lax.optimization_barrier((d_query, d_attn))
    grad_out = t_dot(attended, d_attn)
    grad_query_gain = jnp.sum(d_query * query_hat, axis=0)
    grad_key_gain = jnp.sum(d_key * key_hat, axis=0)
    along = jnp.stack(
        [
            jnp.sum(d_query * gain_query * query_hat, axis=1),
            jnp.sum(d_key * gain_key * key_hat, axis=1),
        ]
    )
    along = ring_sum(along, y)[:, :, None] / D
    along, moe_here = lax.optimization_barrier((along, moe_here))
    d_query = rstd_q * (d_query * gain_query - query_hat * along[0])
    d_key = rstd_k * (d_key * gain_key - key_hat * along[1])
    d_qkv = jnp.concatenate([bf16(d_query), bf16(d_key), bf16(d_value)], axis=1)
    d_par = dot_t(d_qkv, qkv_w[HALF:])
    d_own = dot_t(d_qkv, qkv_w[:HALF])
    grad_norm_attn = jnp.concatenate(
        [
            jnp.sum(d_own * (x_own_all * rstd_one), axis=0),
            jnp.sum(d_par * (x_par_all * rstd_one), axis=0),
        ]
    )
    d_par = bf16(d_par)
    received = other_core(d_par)
    received, d_qkv = lax.optimization_barrier((received, d_qkv))
    d_sent = bf16(d_own + f32(received))
    got = y_scatter([d_sent[s * 256 : s * 256 + 256] for s in range(4)])
    grad_qkv = bf16(t_dot(normed_one, d_qkv))
    got, moe_here = lax.optimization_barrier((got, moe_here))
    layer_output = from_half(bf16(after + moe_here), zh, c)[None]
    d_normed_one = sum(f32(g) for g in got) * gain_attn[0]
    hat_here = x_here * rstd_one[:256]
    along = jnp.sum(d_normed_one * hat_here, axis=1)
    along = (along + other_core(along))[:, None] / D
    grad_tokens = bf16(d_after + rstd_one[:256] * (d_normed_one - hat_here * along))

    wide = jnp.concatenate([grad_norm_moe[:, None], grad_router], axis=1)
    wide = jnp.pad(wide, ((0, HALF), (0, 0)))
    extras = jnp.concatenate([grad_norm_attn[:, None], wide], axis=1).reshape(2, HALF, 18)
    extras = jnp.where(own_first, extras, extras[::-1]).reshape(2, 4, 2, 4, 2, 16, 18)
    gains = jnp.stack([grad_query_gain, grad_key_gain], axis=1)
    at_home = jnp.arange(8)[:, None, None] == head_block
    gains = jnp.where(at_home, gains[None], 0.0).reshape(4, 2, 2, 4, 2, 16, 2)
    extras = jnp.concatenate(
        [extras.transpose(2, 0, 3, 1, 4, 5, 6), gains.transpose(1, 2, 3, 0, 4, 5, 6)], axis=-1
    )
    coarse = bf16(extras)
    extras = jnp.concatenate([coarse, bf16(extras - f32(coarse))], axis=-1)
    extras = jnp.pad(extras, ((0, 0),) * 6 + ((0, 88),))
    both = grad_qkv.reshape(2, HALF, 768)
    both = jnp.where(own_first, both, both[::-1]).reshape(2, 4, 2, 4, 2, 16, 768)
    both = both.transpose(2, 0, 3, 1, 4, 5, 6)
    both = jnp.concatenate([both, extras], axis=-1).reshape(16, 128, 896)
    grad_out = bf16(grad_out).reshape(2, 256, HALF)
    grad_out = jnp.where(own_first, grad_out, grad_out[::-1]).reshape(16, 32, 4, 256)
    grad_out = grad_out.transpose(0, 2, 1, 3).reshape(16, 128, 256)
    both = jnp.concatenate([both, grad_out], axis=2).reshape(D, 1152)
    both, expert_grads, got = lax.optimization_barrier((both, expert_grads, got))
    both = lax.psum_scatter(both, plane, scatter_dimension=0, tiled=True)
    grad_out = both[:, 896:].reshape(4, 32, 256).transpose(1, 0, 2).reshape(32, HALF)
    both = f32(trade(both[:, :896].reshape(8, 16, 896), y, c))
    grad_w_qkv = both[:, :, :768].reshape(8, 16, 3, 256).transpose(1, 2, 0, 3).reshape(16, 3 * D)
    smalls = jnp.sum(both[:, :, 768:788] + both[:, :, 788:808], axis=0)

    out_own = jnp.where(own_first, grad_out[:16], grad_out[16:])
    out_par = other_core(jnp.where(own_first, grad_out[16:], grad_out[:16]))
    grad_w_out = jnp.where(own_first, join_halves(out_own, out_par), join_halves(out_par, out_own))
    grad_w_out = f32(grad_w_out)

    expert_grads = [f32(g) for g in expert_grads]
    grad_gate_up = jnp.stack([g[:, : 2 * FF] for g in expert_grads])
    grad_down = jnp.stack([g[:, 2 * FF :].T for g in expert_grads])
    return (
        layer_output,
        from_half(grad_tokens, zh, c)[None],
        grad_w_qkv,
        grad_w_out,
        smalls[:, 2:18],
        smalls[:, 0],
        smalls[:, 1],
        smalls[:, 18],
        smalls[:, 19],
        grad_gate_up,
        grad_down,
    )


def solution(mesh):
    fine = Mesh(mesh.devices.reshape(4, 2, 2, 4, 2), ("y", "zh", "zl", "x", "c"))
    ctx, fsdp = ("y", "zh"), ("zl", "x", "c")
    rows, blocks, line = P(ctx + fsdp, None), P(fsdp, ctx, None), P(ctx + fsdp)
    gate_up, down = P(ctx, fsdp, None), P(ctx, None, fsdp)
    return jax.shard_map(
        on_device,
        mesh=fine,
        in_specs=(blocks, blocks, rows, rows, rows, line, line, line, line, gate_up, down)
        + (P(fsdp, None, None), P(fsdp, ctx)),
        out_specs=(blocks, blocks, rows, rows, rows, line, line, line, line, gate_up, down),
        check_vma=False,
    )
```

profile of v0, /device:TPU:32, one launch (start us, length us, event | category | flops | bytes accessed | tf_op | source)
XLA Modules:
  0.0 677.9 jit_solution(10115331548505023827)
XLA Ops:
  32.8 4.8 collective-permute-done.1
  63.1 19.2 %collective-permute-done.6 = bf16[256,1024]{0,1:T(8,128)(2,1)S(1)} collective-permute-done((bf16[256,1024]{0,1:T(8,128)(2,1)S(1)}, bf16[256,1024]{0,1:T(8,128)(2,1)S(1)}, u32[]{:S(2)}, u32[]{:S(2)}) %collective-permute-start.6) | collective-permute-done | bytes 524320 | tf_op jit(solution)/shard_map/ppermute | solution.py:44
  133.2 5.0 fusion.199
  138.2 4.4 fusion.123
  156.2 9.1 %collective-permute-done.31 = bf16[256,1024]{0,1:T(8,128)(2,1)S(1)} collective-permute-done((bf16[256,1024]{0,1:T(8,128)(2,1)}, bf16[256,1024]{0,1:T(8,128)(2,1)S(1)}, u32[]{:S(2)}, u32[]{:S(2)}) %collective-permute-start.31) | collective-permute-done | bytes 524320 | tf_op jit(solution)/shard_map/ppermute | solution.py:44
  165.3 12.4 %collective-permute-done.30 = bf16[256,1024]{0,1:T(8,128)(2,1)S(1)} collective-permute-done((bf16[256,1024]{0,1:T(8,128)(2,1)S(1)}, bf16[256,1024]{0,1:T(8,128)(2,1)S(1)}, u32[]{:S(2)}, u32[]{:S(2)}) %collective-permute-start.30) | collective-permute-done | bytes 524320 | tf_op jit(solution)/shard_map/ppermute | solution.py:44
  183.8 21.7 %collective-permute-done.36 = bf16[256,1024]{0,1:T(8,128)(2,1)S(1)} collective-permute-done((bf16[256,1024]{0,1:T(8,128)(2,1)S(1)}, bf16[256,1024]{0,1:T(8,128)(2,1)S(1)}, u32[]{:S(2)}, u32[]{:S(2)}) %collective-permute-start.36) | collective-permute-done | bytes 524320 | tf_op jit(solution)/shard_map/ppermute | solution.py:44
  214.2 5.4 multiply_convert_fusion.5
  219.6 4.6 fusion.106
  224.2 7.2 %fusion.60 = bf16[2,384,2048]{2,1,0:T(8,128)(2,1)S(1)} fusion(bf16[2,384,1024]{2,1,0:T(8,128)(2,1)S(1)} %copy-done.118, bf16[2,1024,3072]{2,1,0:T(8,128)(2,1)} %bitcast.477), kind=kOutput, calls=%fused_computation.70 | convolution fusion | flops 3222798336 | bytes 13107200 | tf_op jit(solution)/shard_map/hsd,hdf->hsf/dot_general | solution.py:163
  239.7 5.5 multiply_convert_fusion.10
  245.2 31.2 %all-gather.6.cloned.1.call-done = bf16[2048,3072]{1,0:T(8,128)(2,1)} async-done(((bf16[128,3072]{1,0:T(8,128)(2,1)}), bf16[2048,3072]{1,0:T(8,128)(2,1)}) %all-gather.6.cloned.1.call-update) | async-done | bytes 12582928 | tf_op jit(solution)/shard_map/all_gather | solution.py:267
  276.3 4.6 fusion.103
  280.9 7.6 %fusion.57 = bf16[2,384,2048]{2,1,0:T(8,128)(2,1)S(1)} fusion(bf16[2,384,1024]{2,1,0:T(8,128)(2,1)S(1)} %copy-done.117, bf16[2,1024,3072]{2,1,0:T(8,128)(2,1)} %bitcast.481), kind=kOutput, calls=%fused_computation.69 | convolution fusion | flops 3222798336 | bytes 13107200 | tf_op jit(solution)/shard_map/hsd,hdf->hsf/dot_general | solution.py:163
  292.1 5.2 convert_add_fusion
  303.4 8.6 %fusion.112 = bf16[2,384,1024]{2,1,0:T(8,128)(2,1)} fusion(bf16[2,1024,3072]{2,1,0:T(8,128)(2,1)} %bitcast.478, bf16[2,384,1024]{2,1,0:T(8,128)(2,1)} %copy-done.13, bf16[2,384,1024]{2,1,0:T(8,128)(2,1)S(1)} %get-tuple-element.216), kind=kOutput, calls=%fused_computation.132 | convolution fusion | flops 3228303360 | bytes 13107200 | tf_op jit(solution)/shard_map/hsf,hdf->hsd/dot_general | solution.py:163
  312.0 5.2 convert_add_fusion.1
  320.5 5.5 multiply_reduce_fusion.3
  326.0 15.9 %fusion.22 = bf16[2,1024,3072]{2,1,0:T(8,128)(2,1)} fusion(bf16[2,384,1024]{2,1,0:T(8,128)(2,1)} %get-tuple-element.215, bf16[2,384,2048]{2,1,0:T(8,128)(2,1)} %pad_maximum_fusion.6, bf16[2,384,1024]{2,1,0:T(8,128)(2,1)} %get-tuple-element.389, bf16[2,384,1024]{2,1,0:T(8,128)(2,1)} %fusion.93), kind=kOutput, calls=%fused_computation.24 | convolution fusion | flops 9714008064 | bytes 20447232 | tf_op jit(solution)/shard_map/hsd,hsf->hdf/dot_general | solution.py:163
  342.0 7.4 %fusion.109 = bf16[2,384,1024]{2,1,0:T(8,128)(2,1)S(1)} fusion(bf16[2,1024,3072]{2,1,0:T(8,128)(2,1)} %bitcast.482, bf16[2,384,1024]{2,1,0:T(8,128)(2,1)} %get-tuple-element.220, bf16[2,384,1024]{2,1,0:T(8,128)(2,1)S(1)} %get-tuple-element.219), kind=kOutput, calls=%fused_computation.131 | convolution fusion | flops 3228303360 | bytes 13107200 | tf_op jit(solution)/shard_map/hsf,hdf->hsd/dot_general | solution.py:163
  357.3 5.5 bitcast_add_fusion
  377.8 23.3 %collective-permute-done.42 = bf16[256,1024]{0,1:T(8,128)(2,1)S(1)} collective-permute-done((bf16[256,1024]{0,1:T(8,128)(2,1)S(1)}, bf16[256,1024]{0,1:T(8,128)(2,1)S(1)}, u32[]{:S(2)}, u32[]{:S(2)}) %collective-permute-start.42) | collective-permute-done | bytes 524320 | tf_op jit(solution)/shard_map/ppermute | solution.py:44
  408.8 21.7 %collective-permute-done.50 = bf16[256,1024]{0,1:T(8,128)(2,1)S(1)} collective-permute-done((bf16[256,1024]{0,1:T(8,128)(2,1)S(1)}, bf16[256,1024]{0,1:T(8,128)(2,1)S(1)}, u32[]{:S(2)}, u32[]{:S(2)}) %collective-permute-start.50) | collective-permute-done | bytes 524320 | tf_op jit(solution)/shard_map/ppermute | solution.py:44
  437.2 16.1 %fusion.19 = bf16[2,1024,3072]{2,1,0:T(8,128)(2,1)} fusion(bf16[2,384,1024]{2,1,0:T(8,128)(2,1)} %get-tuple-element.92, bf16[2,384,2048]{2,1,0:T(8,128)(2,1)} %pad_maximum_fusion.5, bf16[2,384,1024]{2,1,0:T(8,128)(2,1)} %get-tuple-element.90, bf16[2,384,1024]{2,1,0:T(8,128)(2,1)} %fusion.98), kind=kOutput, calls=%fused_computation.23 | convolution fusion | flops 9714008064 | bytes 20447232 | tf_op jit(solution)/shard_map/hsd,hsf->hdf/dot_general | solution.py:163
  469.3 5.1 multiply_reduce_fusion
  483.4 5.4 collective-permute-done.57
  495.9 6.3 fusion.126
  507.3 6.0 fusion.45
  535.0 5.5 convolution_convert_fusion
  542.0 14.3 %collective-permute-done.60 = bf16[256,1024]{0,1:T(8,128)(2,1)S(1)} collective-permute-done((bf16[256,1024]{0,1:T(8,128)(2,1)S(1)}, bf16[256,1024]{0,1:T(8,128)(2,1)S(1)}, u32[]{:S(2)}, u32[]{:S(2)}) %collective-permute-start.60) | collective-permute-done | bytes 524320 | tf_op jit(solution)/shard_map/ppermute | solution.py:44
  565.1 6.4 collective-permute-done.63
  588.2 66.3 %reduce-scatter.8.cloned.1.call-done = bf16[128,1152]{1,0:T(8,128)(2,1)} async-done(((bf16[2048,1152]{1,0:T(8,128)(2,1)}), bf16[128,1152]{1,0:T(8,128)(2,1)}) %reduce-scatter.8.cloned.1.call-update) | async-done | bytes 294928 | tf_op jit(solution)/shard_map/reduce_scatter | solution.py:463
  (723 shorter events, 287.7 us)
Async XLA Ops:
  7.2 84.7 %all-gather.4.cloned.1.call-start = ((), (), s32[]{:S(2)}) async-start(), calls=%async_computation.3 | async-start | bytes 5013504 | tf_op jit(solution)/shard_map/all_gather | solution.py:263
  37.8 181.8 %all-gather.8.cloned.1.call-start = ((), (), s32[]{:S(2)}) async-start(), calls=%async_computation.5 | async-start | bytes 13369344 | tf_op jit(solution)/shard_map/all_gather | solution.py:267
  39.2 237.1 %all-gather.6.cloned.1.call-start = ((), (), s32[]{:S(2)}) async-start(), calls=%async_computation.4 | async-start | bytes 13369344 | tf_op jit(solution)/shard_map/all_gather | solution.py:267
  40.4 416.4 %reduce-scatter.10.cloned.1.call-start = ((), (), s32[]{:S(2)}) async-start(), calls=%async_computation.7 | async-start | bytes 13369344
  54.9 27.9 %collective-permute-start.4 = (bf16[256,1024]{0,1:T(8,128)(2,1)S(1)}, bf16[256,1024]{0,1:T(8,128)(2,1)S(1)}, u32[]{:S(2)}, u32[]{:S(2)}) collective-permute-start(bf16[256,1024]{0,1:T(8,128)(2,1)S(1)} %pad_maximum_fusion.21), channel_id=1, source_target_pairs={{0,32},{32,64},{64,96},{96,0},{1,33},{33,65},{65,97},{97,1},{2,34}... | collective-permute-start | bytes 1572872 | tf_op jit(solution)/shard_map/ppermute | solution.py:44
  55.8 26.5 %collective-permute-start.5 = (bf16[256,1024]{0,1:T(8,128)(2,1)S(1)}, bf16[256,1024]{0,1:T(8,128)(2,1)S(1)}, u32[]{:S(2)}, u32[]{:S(2)}) collective-permute-start(bf16[256,1024]{0,1:T(8,128)(2,1)S(1)} %pad_maximum_fusion.21), channel_id=1, source_target_pairs={{0,64},{32,96},{64,0},{96,32},{1,65},{33,97},{65,1},{97,33},{2,66}... | collective-permute-start | bytes 1572872 | tf_op jit(solution)/shard_map/ppermute | solution.py:44
  58.5 23.9 %collective-permute-start.6 = (bf16[256,1024]{0,1:T(8,128)(2,1)S(1)}, bf16[256,1024]{0,1:T(8,128)(2,1)S(1)}, u32[]{:S(2)}, u32[]{:S(2)}) collective-permute-start(bf16[256,1024]{0,1:T(8,128)(2,1)S(1)} %pad_maximum_fusion.21), channel_id=1, source_target_pairs={{0,96},{32,0},{64,32},{96,64},{1,97},{33,1},{65,33},{97,65},{2,98}... | collective-permute-start | bytes 1572872 | tf_op jit(solution)/shard_map/ppermute | solution.py:44
  59.1 23.9 %collective-permute-start.3 = (bf16[128,1024]{0,1:T(8,128)(2,1)S(1)}, bf16[128,1024]{0,1:T(8,128)(2,1)S(1)}, u32[]{:S(2)}, u32[]{:S(2)}) collective-permute-start(bf16[128,1024]{0,1:T(8,128)(2,1)S(1)} %broadcast_select_fusion.13), channel_id=1, source_target_pairs={{0,16},{16,0},{1,17},{17,1},{2,18},{18,2},{3,19},{19,3},{4,20},{20... | collective-permute-start | bytes 786440 | tf_op jit(solution)/shard_map/ppermute | solution.py:107
  63.1 22.2 %collective-permute-start.7 = (bf16[256,1024]{0,1:T(8,128)(2,1)S(1)}, bf16[256,1024]{0,1:T(8,128)(2,1)S(1)}, u32[]{:S(2)}, u32[]{:S(2)}) collective-permute-start(bf16[256,1024]{0,1:T(8,128)(2,1)S(1)} %pad_maximum_fusion.21), channel_id=1, source_target_pairs={{0,1},{1,0},{2,3},{3,2},{4,5},{5,4},{6,7},{7,6},{8,9},{9,8},{10,11... | collective-permute-start | bytes 1572872 | tf_op jit(solution)/shard_map/ppermute | solution.py:40
  84.1 58.5 %collective-permute-start.25 = (bf16[256,1024]{0,1:T(8,128)(2,1)}, bf16[256,1024]{0,1:T(8,128)(2,1)}, u32[]{:S(2)}, u32[]{:S(2)}) collective-permute-start(bf16[256,1024]{0,1:T(8,128)(2,1)} %pad_maximum_fusion.22), channel_id=1, source_target_pairs={{0,32},{32,64},{64,96},{96,0},{1,33},{33,65},{65,97},{97,1},{2,34}... | collective-permute-start | bytes 1572872 | tf_op jit(solution)/shard_map/ppermute | solution.py:44
  85.4 57.2 %collective-permute-start.26 = (bf16[256,1024]{0,1:T(8,128)(2,1)}, bf16[256,1024]{0,1:T(8,128)(2,1)}, u32[]{:S(2)}, u32[]{:S(2)}) collective-permute-start(bf16[256,1024]{0,1:T(8,128)(2,1)} %pad_maximum_fusion.22), channel_id=1, source_target_pairs={{0,64},{32,96},{64,0},{96,32},{1,65},{33,97},{65,1},{97,33},{2,66}... | collective-permute-start | bytes 1572872 | tf_op jit(solution)/shard_map/ppermute | solution.py:44
  151.1 26.6 %collective-permute-start.30 = (bf16[256,1024]{0,1:T(8,128)(2,1)S(1)}, bf16[256,1024]{0,1:T(8,128)(2,1)S(1)}, u32[]{:S(2)}, u32[]{:S(2)}) collective-permute-start(bf16[256,1024]{0,1:T(8,128)(2,1)S(1)} %get-tuple-element.242), channel_id=1, source_target_pairs={{0,64},{32,96},{64,0},{96,32},{1,65},{33,97},{65,1},{97,33},{2,66}... | collective-permute-start | bytes 1572872 | tf_op jit(solution)/shard_map/ppermute | solution.py:44
  154.3 23.4 %collective-permute-start.29 = (bf16[256,1024]{0,1:T(8,128)(2,1)S(1)}, bf16[256,1024]{0,1:T(8,128)(2,1)S(1)}, u32[]{:S(2)}, u32[]{:S(2)}) collective-permute-start(bf16[256,1024]{0,1:T(8,128)(2,1)S(1)} %get-tuple-element.240), channel_id=1, source_target_pairs={{0,96},{32,0},{64,32},{96,64},{1,97},{33,1},{65,33},{97,65},{2,98}... | collective-permute-start | bytes 1572872 | tf_op jit(solution)/shard_map/ppermute | solution.py:44
  180.7 24.7 %collective-permute-start.36 = (bf16[256,1024]{0,1:T(8,128)(2,1)S(1)}, bf16[256,1024]{0,1:T(8,128)(2,1)S(1)}, u32[]{:S(2)}, u32[]{:S(2)}) collective-permute-start(bf16[256,1024]{0,1:T(8,128)(2,1)S(1)} %multiply_convert_fusion.13), channel_id=1, source_target_pairs={{0,96},{32,0},{64,32},{96,64},{1,97},{33,1},{65,33},{97,65},{2,98}... | collective-permute-start | bytes 1572872 | tf_op jit(solution)/shard_map/ppermute | solution.py:44
  182.7 22.8 %collective-permute-start.35 = (bf16[256,1024]{0,1:T(8,128)(2,1)S(1)}, bf16[256,1024]{0,1:T(8,128)(2,1)S(1)}, u32[]{:S(2)}, u32[]{:S(2)}) collective-permute-start(bf16[256,1024]{0,1:T(8,128)(2,1)S(1)} %multiply_convert_fusion.13), channel_id=1, source_target_pairs={{0,64},{32,96},{64,0},{96,32},{1,65},{33,97},{65,1},{97,33},{2,66}... | collective-permute-start | bytes 1572872 | tf_op jit(solution)/shard_map/ppermute | solution.py:44
  183.0 25.9 %collective-permute-start.34 = (bf16[256,1024]{0,1:T(8,128)(2,1)S(1)}, bf16[256,1024]{0,1:T(8,128)(2,1)S(1)}, u32[]{:S(2)}, u32[]{:S(2)}) collective-permute-start(bf16[256,1024]{0,1:T(8,128)(2,1)S(1)} %multiply_convert_fusion.13), channel_id=1, source_target_pairs={{0,32},{32,64},{64,96},{96,0},{1,33},{33,65},{65,97},{97,1},{2,34}... | collective-permute-start | bytes 1572872 | tf_op jit(solution)/shard_map/ppermute | solution.py:44
  234.8 57.3 %collective-permute-start.39 = (bf16[2,384,3072]{2,1,0:T(8,128)(2,1)}, bf16[2,384,3072]{2,1,0:T(8,128)(2,1)}, u32[]{:S(2)}, u32[]{:S(2)}) collective-permute-start(bf16[2,384,3072]{2,1,0:T(8,128)(2,1)} %pad_maximum_fusion.1), channel_id=1, source_target_pairs={{0,1},{1,0},{2,3},{3,2},{4,5},{5,4},{6,7},{7,6},{8,9},{9,8},{10,11... | collective-permute-start | bytes 14155784 | tf_op jit(solution)/shard_map/ppermute | solution.py:40
  291.7 20.3 %collective-permute-start.38 = (bf16[2,384,3072]{2,1,0:T(8,128)(2,1)}, bf16[2,384,3072]{2,1,0:T(8,128)(2,1)}, u32[]{:S(2)}, u32[]{:S(2)}) collective-permute-start(bf16[2,384,3072]{2,1,0:T(8,128)(2,1)} %pad_maximum_fusion), channel_id=1, source_target_pairs={{0,1},{1,0},{2,3},{3,2},{4,5},{5,4},{6,7},{7,6},{8,9},{9,8},{10,11... | collective-permute-start | bytes 14155784 | tf_op jit(solution)/shard_map/ppermute | solution.py:40
  362.8 214.1 %reduce-scatter.12.cloned.1.call-start = ((), (), s32[]{:S(2)}) async-start(), calls=%async_computation.8 | async-start | bytes 13369344
  374.3 26.8 %collective-permute-start.42 = (bf16[256,1024]{0,1:T(8,128)(2,1)S(1)}, bf16[256,1024]{0,1:T(8,128)(2,1)S(1)}, u32[]{:S(2)}, u32[]{:S(2)}) collective-permute-start(bf16[256,1024]{0,1:T(8,128)(2,1)S(1)} %get-tuple-element.224), channel_id=1, source_target_pairs={{0,32},{32,64},{64,96},{96,0},{1,33},{33,65},{65,97},{97,1},{2,34}... | collective-permute-start | bytes 1572872 | tf_op jit(solution)/shard_map/ppermute | solution.py:44
  375.0 26.1 %collective-permute-start.41 = (bf16[256,1024]{0,1:T(8,128)(2,1)S(1)}, bf16[256,1024]{0,1:T(8,128)(2,1)S(1)}, u32[]{:S(2)}, u32[]{:S(2)}) collective-permute-start(bf16[256,1024]{0,1:T(8,128)(2,1)S(1)} %get-tuple-element.223), channel_id=1, source_target_pairs={{0,64},{32,96},{64,0},{96,32},{1,65},{33,97},{65,1},{97,33},{2,66}... | collective-permute-start | bytes 1572872 | tf_op jit(solution)/shard_map/ppermute | solution.py:44
  377.0 24.7 %collective-permute-start.40 = (bf16[256,1024]{0,1:T(8,128)(2,1)S(1)}, bf16[256,1024]{0,1:T(8,128)(2,1)S(1)}, u32[]{:S(2)}, u32[]{:S(2)}) collective-permute-start(bf16[256,1024]{0,1:T(8,128)(2,1)S(1)} %get-tuple-element.222), channel_id=1, source_target_pairs={{0,96},{32,0},{64,32},{96,64},{1,97},{33,1},{65,33},{97,65},{2,98}... | collective-permute-start | bytes 1572872 | tf_op jit(solution)/shard_map/ppermute | solution.py:44
  405.2 25.3 %collective-permute-start.50 = (bf16[256,1024]{0,1:T(8,128)(2,1)S(1)}, bf16[256,1024]{0,1:T(8,128)(2,1)S(1)}, u32[]{:S(2)}, u32[]{:S(2)}) collective-permute-start(bf16[256,1024]{0,1:T(8,128)(2,1)S(1)} %get-tuple-element.205), channel_id=1, source_target_pairs={{0,96},{32,0},{64,32},{96,64},{1,97},{33,1},{65,33},{97,65},{2,98}... | collective-permute-start | bytes 1572872 | tf_op jit(solution)/shard_map/ppermute | solution.py:44
  407.7 22.8 %collective-permute-start.49 = (bf16[256,1024]{0,1:T(8,128)(2,1)S(1)}, bf16[256,1024]{0,1:T(8,128)(2,1)S(1)}, u32[]{:S(2)}, u32[]{:S(2)}) collective-permute-start(bf16[256,1024]{0,1:T(8,128)(2,1)S(1)} %get-tuple-element.205), channel_id=1, source_target_pairs={{0,64},{32,96},{64,0},{96,32},{1,65},{33,97},{65,1},{97,33},{2,66}... | collective-permute-start | bytes 1572872 | tf_op jit(solution)/shard_map/ppermute | solution.py:44
  407.7 26.2 %collective-permute-start.48 = (bf16[256,1024]{0,1:T(8,128)(2,1)S(1)}, bf16[256,1024]{0,1:T(8,128)(2,1)S(1)}, u32[]{:S(2)}, u32[]{:S(2)}) collective-permute-start(bf16[256,1024]{0,1:T(8,128)(2,1)S(1)} %get-tuple-element.205), channel_id=1, source_target_pairs={{0,32},{32,64},{64,96},{96,0},{1,33},{33,65},{65,97},{97,1},{2,34}... | collective-permute-start | bytes 1572872 | tf_op jit(solution)/shard_map/ppermute | solution.py:44
  459.2 195.3 %reduce-scatter.8.cloned.1.call-start = ((), (), s32[]{:S(2)}) async-start(), calls=%async_computation.6 | async-start | bytes 5013504 | tf_op jit(solution)/shard_map/reduce_scatter | solution.py:463
  462.3 21.0 %collective-permute-start.58 = (bf16[256,1024]{0,1:T(8,128)(2,1)}, bf16[256,1024]{0,1:T(8,128)(2,1)}, u32[]{:S(2)}, u32[]{:S(2)}) collective-permute-start(bf16[256,1024]{0,1:T(8,128)(2,1)} %get-tuple-element.238), channel_id=1, source_target_pairs={{0,32},{32,64},{64,96},{96,0},{1,33},{33,65},{65,97},{97,1},{2,34}... | collective-permute-start | bytes 1572872 | tf_op jit(solution)/shard_map/ppermute | solution.py:44
  463.9 24.9 %collective-permute-start.57 = (bf16[256,1024]{0,1:T(8,128)(2,1)}, bf16[256,1024]{0,1:T(8,128)(2,1)}, u32[]{:S(2)}, u32[]{:S(2)}) collective-permute-start(bf16[256,1024]{0,1:T(8,128)(2,1)} %get-tuple-element.239), channel_id=1, source_target_pairs={{0,64},{32,96},{64,0},{96,32},{1,65},{33,97},{65,1},{97,33},{2,66}... | collective-permute-start | bytes 1572872 | tf_op jit(solution)/shard_map/ppermute | solution.py:44
  466.6 22.5 %collective-permute-start.56 = (bf16[256,1024]{0,1:T(8,128)(2,1)}, bf16[256,1024]{0,1:T(8,128)(2,1)}, u32[]{:S(2)}, u32[]{:S(2)}) collective-permute-start(bf16[256,1024]{0,1:T(8,128)(2,1)} %get-tuple-element.237), channel_id=1, source_target_pairs={{0,96},{32,0},{64,32},{96,64},{1,97},{33,1},{65,33},{97,65},{2,98}... | collective-permute-start | bytes 1572872 | tf_op jit(solution)/shard_map/ppermute | solution.py:44
  530.2 26.1 %collective-permute-start.60 = (bf16[256,1024]{0,1:T(8,128)(2,1)S(1)}, bf16[256,1024]{0,1:T(8,128)(2,1)S(1)}, u32[]{:S(2)}, u32[]{:S(2)}) collective-permute-start(bf16[256,1024]{0,1:T(8,128)(2,1)S(1)} %get-tuple-element.235), channel_id=1, source_target_pairs={{0,96},{32,0},{64,32},{96,64},{1,97},{33,1},{65,33},{97,65},{2,98}... | collective-permute-start | bytes 1572872 | tf_op jit(solution)/shard_map/ppermute | solution.py:44
  533.6 22.8 %collective-permute-start.61 = (bf16[256,1024]{0,1:T(8,128)(2,1)S(1)}, bf16[256,1024]{0,1:T(8,128)(2,1)S(1)}, u32[]{:S(2)}, u32[]{:S(2)}) collective-permute-start(bf16[256,1024]{0,1:T(8,128)(2,1)S(1)} %get-tuple-element.234), channel_id=1, source_target_pairs={{0,64},{32,96},{64,0},{96,32},{1,65},{33,97},{65,1},{97,33},{2,66}... | collective-permute-start | bytes 1572872 | tf_op jit(solution)/shard_map/ppermute | solution.py:44
  534.8 25.2 %collective-permute-start.62 = (bf16[256,1024]{0,1:T(8,128)(2,1)S(1)}, bf16[256,1024]{0,1:T(8,128)(2,1)S(1)}, u32[]{:S(2)}, u32[]{:S(2)}) collective-permute-start(bf16[256,1024]{0,1:T(8,128)(2,1)S(1)} %get-tuple-element.233), channel_id=1, source_target_pairs={{0,32},{32,64},{64,96},{96,0},{1,33},{33,65},{65,97},{97,1},{2,34}... | collective-permute-start | bytes 1572872 | tf_op jit(solution)/shard_map/ppermute | solution.py:44
  (169 other events, 1607.3 us)
Sparse Core Ops, SparseCore 0:
  37.9 53.9 all-gather.3
  94.7 89.7 all-gather.7
  186.6 89.6 all-gather.5
  362.9 93.9 reduce-scatter.9
  460.1 93.3 reduce-scatter.11
  578.6 75.8 reduce-scatter.7
where the time goes:
time: 689 us; the launch traced here: 678 us
  waiting for transfers between devices  275 us (40%)
  matrix products  159 us (23%)
  starting transfers between devices  81.4 us (12%)
  other arithmetic  76.4 us (11%)
  local copies, waits for them, and re-layouts  69.1 us (10%)
  between operations  17.9 us (3%)
    ppermute x42, waiting for transfers between devices, from_chip(): return lax.ppermute(a, 'y', [(i, (i + step) % 4) for i in range(4)])  152 us
    dot_general x14, matrix products, per_expert(): return jnp.einsum(pattern, a, b, preferred_element_type=jnp.float32)  99.6 us
    reduce_scatter x1, waiting for transfers between devices, on_device(): both = lax.psum_scatter(both, plane, scatter_dimension=0, tiled=True)  66.3 us
    ppermute x42, starting transfers between devices, from_chip(): return lax.ppermute(a, 'y', [(i, (i + step) % 4) for i in range(4)])  62.3 us
    all_gather x2, waiting for transfers between devices, on_device(): lax.all_gather(jnp.concatenate([w_gate_up[m], down_t[m]], axis=1), plane,...  31.2 us
    unnamed x325, local copies, waits for them, and re-layouts  23.6 us
    convert_element_type x13, other arithmetic, bf16(): return a.astype(jnp.bfloat16)  21.5 us
    dot_general x4, matrix products, t_dot(): lax.dot_general(a, b, (((0,), (0,)), ((), ())), preferred_element_type=jn...  17.6 us
  transfers between devices with their start and end apart: 79, of which 37 were waited for; matrix products, arithmetic and copies ran while one was open for 35% of the time, Pallas kernels for 0%

commit v1 on v0

v1 whole, which is shorter than its diff:
```python
import jax
import jax.numpy as jnp
import numpy as np
from jax import lax
from jax.experimental import pallas as pl
from jax.experimental.pallas import tpu as pltpu
from jax.sharding import Mesh, PartitionSpec as P

D = 2048
HALF = 1024
HEAD_DIM = 128
FF = 1024
CAP = 384
ROWS = 128
SCALE = HEAD_DIM**-0.5

epsilon = 1e-06
rope_base = 10000.0


def f32(a):
    return a.astype(jnp.float32)


def bf16(a):
    return a.astype(jnp.bfloat16)


def dot(a, b):
    return jnp.dot(a, b, preferred_element_type=jnp.float32)


def dot_t(a, b):
    return lax.dot_general(a, b, (((1,), (1,)), ((), ())), preferred_element_type=jnp.float32)


def t_dot(a, b):
    return lax.dot_general(a, b, (((0,), (0,)), ((), ())), preferred_element_type=jnp.float32)


def other_core(a):
    return lax.ppermute(a, "c", [(0, 1), (1, 0)])


def from_chip(a, step):
    return lax.ppermute(a, "y", [(i, (i + step) % 4) for i in range(4)])


def y_gather(a):
    return [a] + [from_chip(a, step) for step in (1, 2, 3)]


def y_scatter(parts):
    return [parts[0]] + [from_chip(parts[step], 4 - step) for step in (1, 2, 3)]


def by_distance(a, y):
    place = (y - jnp.arange(4)) % 4
    hit = place[:, None] == jnp.arange(4)[None, :]
    return jnp.sum(jnp.where(hit[None, :, :, None], a[:, None], jnp.zeros((), a.dtype)), axis=2)


def chosen(a, place):
    hit = place[:, None] == jnp.arange(4)[None, :]
    hit = hit.reshape(4, 4, *[1] * (a.ndim - 1))
    return jnp.sum(jnp.where(hit, a[None], jnp.zeros((), a.dtype)), axis=1)


def trade(pieces, y, c):
    pairs = pieces.reshape(4, 2, *pieces.shape[1:])
    mine = jnp.where(c == 0, pairs[:, 0], pairs[:, 1])
    theirs = jnp.where(c == 0, pairs[:, 1], pairs[:, 0])
    got = other_core(theirs)
    both = jnp.where(c == 0, jnp.stack([mine, got], 1), jnp.stack([got, mine], 1))
    both = chosen(both, (y + jnp.arange(4)) % 4)
    got = jnp.stack([both[0]] + [from_chip(both[step], step) for step in (1, 2, 3)])
    return chosen(got, (y - jnp.arange(4)) % 4).reshape(pieces.shape)


def ring_sum(a, y):
    n = a.shape[0]
    a = a + other_core(a)
    a = by_distance(a.reshape(n, 4, 256), y)
    a = a + from_chip(a, 1) + from_chip(a, 2) + from_chip(a, 3)
    return by_distance(a, y).reshape(n, 1024)


def angle_tables():
    frequency = rope_base ** (-2.0 * np.arange(64) / HEAD_DIM)
    blocks = np.arange(8)[:, None] * ROWS * frequency[None]
    rows = np.arange(ROWS)[:, None] * frequency[None]
    tables = (np.cos(blocks), np.sin(blocks), np.cos(rows), np.sin(rows))
    return [jnp.asarray(table, jnp.float32) for table in tables]


def split_halves(a):
    blocks = [a[..., k * 128 : k * 128 + 128] for k in range(a.shape[-1] // 128)]
    return jnp.concatenate(blocks[0::2], axis=-1), jnp.concatenate(blocks[1::2], axis=-1)


def join_halves(low, high):
    blocks = []
    for k in range(low.shape[-1] // 128):
        blocks += [low[..., k * 128 : k * 128 + 128], high[..., k * 128 : k * 128 + 128]]
    return jnp.concatenate(blocks, axis=-1)


def other_layer(a):
    return lax.ppermute(a, "zh", [(0, 1), (1, 0)])


def to_half(low, high, zh, c):
    mine = jnp.where(c == 0, low, high)
    got = other_core(jnp.where(c == 0, high, low))
    keep = jnp.where(zh == c, mine, got)
    got = other_layer(jnp.where(zh == c, got, mine))
    return jnp.where(zh == 0, keep, got), jnp.where(zh == 0, got, keep)


def from_half(a, zh, c):
    first, second = a[:ROWS], a[ROWS:]
    mine = jnp.where(zh == 0, first, second)
    got = other_layer(jnp.where(zh == 0, second, first))
    keep = jnp.where(zh == c, mine, got)
    got = other_core(jnp.where(zh == c, got, mine))
    return join_halves(jnp.where(c == 0, keep, got), jnp.where(c == 0, got, keep))


def roped(values, cosine, sine):
    return values * cosine + pltpu.roll(values, 64, 1) * sine


def project_kernel(*refs):
    own, par = refs[:4], refs[4:8]
    gain, weights, qkv, tokens, rstd, squares = refs[8:]
    for s in range(4):

        @pl.when(pl.program_id(0) == s)
        def _():
            first, second = own[s][...].astype(jnp.float32), par[s][...].astype(jnp.float32)
            tokens[:, pl.ds(0, HALF)] = own[s][...]
            tokens[:, pl.ds(HALF, HALF)] = par[s][...]
            total = jnp.sum(first * first, axis=1, keepdims=True)
            total = total + jnp.sum(second * second, axis=1, keepdims=True)
            scale = lax.rsqrt(total * (1.0 / D) + epsilon)
            rstd[...] = scale
            first = (first * scale * gain[pl.ds(0, 1), :]).astype(jnp.bfloat16)
            second = (second * scale * gain[pl.ds(1, 1), :]).astype(jnp.bfloat16)
            out = dot(first, weights[pl.ds(0, HALF), :])
            out = out + dot(second, weights[pl.ds(HALF, HALF), :])
            qkv[...] = out
            ones = jnp.ones((8, 256), jnp.bfloat16)
            for k in range(2):
                part = out[:, k * 256 : k * 256 + 256]
                part = part * part
                coarse = part.astype(jnp.bfloat16)
                fine = (part - coarse.astype(jnp.float32)).astype(jnp.bfloat16)
                squares[pl.ds(k * 8, 8), :] = dot_t(ones, coarse) + dot_t(ones, fine)


def project(own, par, gain, weights):
    whole = pl.BlockSpec((256, HALF), lambda s: (0, 0))
    rows = lambda n: pl.BlockSpec((256, n), lambda s: (s, 0))
    return pl.pallas_call(
        project_kernel,
        grid=(4,),
        in_specs=[whole] * 8
        + [pl.BlockSpec((2, HALF), lambda s: (0, 0)), pl.BlockSpec((D, 768), lambda s: (0, 0))],
        out_specs=[
            rows(768),
            rows(D),
            rows(1),
            pl.BlockSpec((16, 256), lambda s: (0, s)),
        ],
        out_shape=[
            jax.ShapeDtypeStruct((1024, 768), jnp.float32),
            jax.ShapeDtypeStruct((1024, D), jnp.bfloat16),
            jax.ShapeDtypeStruct((1024, 1), jnp.float32),
            jax.ShapeDtypeStruct((16, 1024), jnp.float32),
        ],
        compiler_params=pltpu.CompilerParams(vmem_limit_bytes=VMEM_LIMIT),
        cost_estimate=pl.CostEstimate(
            flops=2 * 1024 * D * 768, bytes_accessed=20 << 20, transcendentals=0
        ),
    )(*own, *par, gain, weights)


def spread_kernel(
    d_q, d_k, d_v, q_pre, k_pre, rstd_q, rstd_k, along_q, along_k, gain_q, gain_k, tokens, rstd,
    weights, d_qkv, d_par, d_own, d_gain,
):
    @pl.when(pl.program_id(0) == 0)
    def _():
        d_gain[...] = jnp.zeros_like(d_gain)

    sides = (
        (d_q, q_pre, rstd_q, along_q, gain_q),
        (d_k, k_pre, rstd_k, along_k, gain_k),
    )
    for k, (grad, pre, scale, along, gain) in enumerate(sides):
        hat = pre[...] * scale[...]
        part = scale[...] * (grad[...] * gain[...] - hat * along[...])
        d_qkv[:, pl.ds(k * 256, 256)] = part.astype(jnp.bfloat16)
    d_qkv[:, pl.ds(512, 256)] = d_v[0]
    low = d_qkv[...]
    for k, out in ((1, d_par), (0, d_own)):
        at = pl.ds(k * HALF, HALF)
        part = dot_t(low, weights[at, :])
        out[...] = part.astype(out.dtype)
        hat = tokens[:, at].astype(jnp.float32) * rstd[...]
        d_gain[:, at] += jnp.sum(part * hat, axis=0, keepdims=True)


def spread(d_q, d_k, d_v, qkv, rstd_q, rstd_k, along_q, along_k, gain_q, gain_k, tokens, rstd, w):
    rows = lambda n, k=0: pl.BlockSpec((256, n), lambda s: (s, k))
    line = pl.BlockSpec((1, 256), lambda s: (0, 0))
    return pl.pallas_call(
        spread_kernel,
        grid=(4,),
        in_specs=[
            rows(256),
            rows(256),
            pl.BlockSpec((1, 256, 256), lambda s: (s, 0, 0)),
            rows(256),
            rows(256, 1),
            rows(1),
            rows(1),
            rows(1),
            rows(1),
            line,
            line,
            rows(D),
            rows(1),
            pl.BlockSpec((D, 768), lambda s: (0, 0)),
        ],
        out_specs=[rows(768), rows(HALF), rows(HALF), pl.BlockSpec((1, D), lambda s: (0, 0))],
        out_shape=[
            jax.ShapeDtypeStruct((1024, 768), jnp.bfloat16),
            jax.ShapeDtypeStruct((1024, HALF), jnp.bfloat16),
            jax.ShapeDtypeStruct((1024, HALF), jnp.float32),
            jax.ShapeDtypeStruct((1, D), jnp.float32),
        ],
        compiler_params=pltpu.CompilerParams(vmem_limit_bytes=VMEM_LIMIT),
        cost_estimate=pl.CostEstimate(
            flops=2 * 1024 * D * 768, bytes_accessed=20 << 20, transcendentals=0
        ),
    )(
        d_q, d_k, d_v, qkv, qkv, rstd_q, rstd_k, along_q, along_k,
        gain_q[None], gain_k[None], tokens, rstd, w,
    )


def whole_spec(*shape):
    return pl.BlockSpec(shape, lambda *_: (0,) * len(shape))


def params(flops, data):
    return dict(
        compiler_params=pltpu.CompilerParams(vmem_limit_bytes=VMEM_LIMIT),
        cost_estimate=pl.CostEstimate(flops=flops, bytes_accessed=data, transcendentals=0),
    )


def output_kernel(attended, weights, parts, own):
    out = dot(attended[...], weights[...])
    parts[0] = out.astype(jnp.bfloat16)

    @pl.when(pl.program_id(0) == 0)
    def _():
        own[...] = out


def output_product(attended, weights):
    return pl.pallas_call(
        output_kernel,
        grid=(4,),
        in_specs=[pl.BlockSpec((256, 512), lambda s: (s, 0)), whole_spec(512, HALF)],
        out_specs=[pl.BlockSpec((1, 256, HALF), lambda s: (s, 0, 0)), whole_spec(256, HALF)],
        out_shape=[
            jax.ShapeDtypeStruct((4, 256, HALF), jnp.bfloat16),
            jax.ShapeDtypeStruct((256, HALF), jnp.float32),
        ],
        **params(1 << 30, 5 << 20),
    )(attended, weights)


def residual_kernel(tokens, own, first, second, third, after, square):
    total = tokens[...].astype(jnp.float32) + own[...]
    for part in (first, second, third):
        total = total + part[...].astype(jnp.float32)
    after[...] = total
    square[...] = jnp.sum(total * total, axis=1, keepdims=True)


def residual(tokens, own, got):
    rows = whole_spec(256, HALF)
    return pl.pallas_call(
        residual_kernel,
        grid=(1,),
        in_specs=[rows] * 5,
        out_specs=[rows, whole_spec(256, 1)],
        out_shape=[
            jax.ShapeDtypeStruct((256, HALF), jnp.float32),
            jax.ShapeDtypeStruct((256, 1), jnp.float32),
        ],
        **params(1 << 20, 5 << 20),
    )(tokens, own, *got)


def logits_kernel(router_t, normed, out):
    out[...] = dot_t(router_t[...], normed[...])


def logits_of(router_t, normed):
    return pl.pallas_call(
        logits_kernel,
        grid=(1,),
        in_specs=[whole_spec(16, HALF), whole_spec(1024, HALF)],
        out_specs=whole_spec(16, 1024),
        out_shape=jax.ShapeDtypeStruct((16, 1024), jnp.float32),
        **params(1 << 25, 2 << 20),
    )(router_t, normed)


def route_back_kernel(
    normed, d_logits, router_t, after, rstd, gain, *refs
):
    got, (grad, d_normed, d_gain, along) = refs[:4], refs[4:]
    coarse = d_logits[...].astype(jnp.bfloat16)
    fine = (d_logits[...] - coarse.astype(jnp.float32)).astype(jnp.bfloat16)
    grad[...] = dot(coarse, normed[...]) + dot(fine, normed[...])
    total = got[0][...].astype(jnp.float32)
    for part in got[1:]:
        total = total + part[...].astype(jnp.float32)
    total = total + (t_dot(coarse, router_t[...]) + t_dot(fine, router_t[...]))
    d_normed[...] = total
    hat = after[...] * rstd[...]
    d_gain[...] = jnp.sum(total * hat, axis=0, keepdims=True)
    along[...] = jnp.sum(total * gain[...] * hat, axis=1, keepdims=True)


def route_back(normed, d_logits, router_t, after, rstd, gain, got):
    rows = whole_spec(256, HALF)
    return pl.pallas_call(
        route_back_kernel,
        grid=(1,),
        in_specs=[
            rows,
            whole_spec(16, 256),
            whole_spec(16, HALF),
            rows,
            whole_spec(256, 1),
            whole_spec(1, HALF),
            rows,
            rows,
            rows,
            rows,
        ],
        out_specs=[whole_spec(16, HALF), rows, whole_spec(1, HALF), whole_spec(256, 1)],
        out_shape=[
            jax.ShapeDtypeStruct((16, HALF), jnp.float32),
            jax.ShapeDtypeStruct((256, HALF), jnp.float32),
            jax.ShapeDtypeStruct((1, HALF), jnp.float32),
            jax.ShapeDtypeStruct((256, 1), jnp.float32),
        ],
        **params(1 << 25, 6 << 20),
    )(normed, d_logits, router_t, after, rstd, gain, *got)


def back_kernel(tokens, rstd, gain, first, second, third, fourth, d_normed, along):
    total = first[...].astype(jnp.float32)
    for part in (second, third, fourth):
        total = total + part[...].astype(jnp.float32)
    total = total * gain[...]
    d_normed[...] = total
    hat = tokens[...].astype(jnp.float32) * rstd[...]
    along[...] = jnp.sum(total * hat, axis=1, keepdims=True)


def back_sums(tokens, rstd, gain, got):
    rows = whole_spec(256, HALF)
    return pl.pallas_call(
        back_kernel,
        grid=(1,),
        in_specs=[rows, whole_spec(256, 1), whole_spec(1, HALF)] + [rows] * 4,
        out_specs=[rows, whole_spec(256, 1)],
        out_shape=[
            jax.ShapeDtypeStruct((256, HALF), jnp.float32),
            jax.ShapeDtypeStruct((256, 1), jnp.float32),
        ],
        **params(1 << 20, 5 << 20),
    )(tokens, rstd, gain, *got)


def out_grad_kernel(attended, d_attn, out, total):
    @pl.when(pl.program_id(0) == 0)
    def _():
        total[...] = jnp.zeros_like(total)

    total[...] += t_dot(attended[...], d_attn[...])

    @pl.when(pl.program_id(0) == 3)
    def _():
        out[...] = total[...].astype(jnp.bfloat16)


def out_grad(attended, d_attn):
    rows = lambda n: pl.BlockSpec((256, n), lambda s: (s, 0))
    return pl.pallas_call(
        out_grad_kernel,
        grid=(4,),
        in_specs=[rows(512), rows(HALF)],
        out_specs=whole_spec(512, HALF),
        out_shape=jax.ShapeDtypeStruct((512, HALF), jnp.bfloat16),
        scratch_shapes=[pltpu.VMEM((512, HALF), jnp.float32)],
        **params(1 << 30, 5 << 20),
    )(attended, d_attn)


def heads_kernel(d_attn, weights, own, par):
    own[...] = dot_t(d_attn[...], weights[pl.ds(0, 256), :])
    par[...] = dot_t(d_attn[...], weights[pl.ds(256, 256), :])


def heads_product(d_attn, weights):
    rows = lambda n: pl.BlockSpec((256, n), lambda s: (s, 0))
    return pl.pallas_call(
        heads_kernel,
        grid=(4,),
        in_specs=[rows(HALF), whole_spec(512, HALF)],
        out_specs=[rows(256), rows(256)],
        out_shape=[jax.ShapeDtypeStruct((1024, 256), jnp.float32)] * 2,
        **params(1 << 30, 5 << 20),
    )(d_attn, weights)


def along_kernel(
    d_q, d_k, q_pre, k_pre, rstd_q, rstd_k, gain_q, gain_k, along, d_gain_q, d_gain_k
):
    @pl.when(pl.program_id(0) == 0)
    def _():
        d_gain_q[...] = jnp.zeros_like(d_gain_q)
        d_gain_k[...] = jnp.zeros_like(d_gain_k)

    ones = jnp.ones((8, 256), jnp.bfloat16)
    sides = ((d_q, q_pre, rstd_q, gain_q, d_gain_q), (d_k, k_pre, rstd_k, gain_k, d_gain_k))
    for k, (grad, pre, scale, gain, d_gain) in enumerate(sides):
        part = grad[...] * (pre[...] * scale[...])
        d_gain[...] += jnp.sum(part, axis=0, keepdims=True)
        part = part * gain[...]
        coarse = part.astype(jnp.bfloat16)
        part = part - coarse.astype(jnp.float32)
        fine = part.astype(jnp.bfloat16)
        along[pl.ds(k * 8, 8), :] = dot_t(ones, coarse) + dot_t(ones, fine)


def along_sums(d_q, d_k, qkv, rstd_q, rstd_k, gain_q, gain_k):
    rows = lambda n, k=0: pl.BlockSpec((256, n), lambda s: (s, k))
    line = whole_spec(1, 256)
    return pl.pallas_call(
        along_kernel,
        grid=(4,),
        in_specs=[rows(256), rows(256), rows(256), rows(256, 1), rows(1), rows(1), line, line],
        out_specs=[pl.BlockSpec((16, 256), lambda s: (0, s)), line, line],
        out_shape=[
            jax.ShapeDtypeStruct((16, 1024), jnp.float32),
            jax.ShapeDtypeStruct((1, 256), jnp.float32),
            jax.ShapeDtypeStruct((1, 256), jnp.float32),
        ],
        **params(1 << 22, 5 << 20),
    )(d_q, d_k, qkv, qkv, rstd_q, rstd_k, gain_q[None], gain_k[None])


def outer_kernel(tokens, rstd, gain, d_qkv, out, total):
    @pl.when(pl.program_id(0) == 0)
    def _():
        total[...] = jnp.zeros_like(total)

    low = d_qkv[...]
    for k in range(4):
        at = pl.ds(k * 512, 512)
        normed = tokens[:, at].astype(jnp.float32) * rstd[...] * gain[:, at]
        total[at, :] += dot(jnp.transpose(normed).astype(jnp.bfloat16), low)

    @pl.when(pl.program_id(0) == 3)
    def _():
        out[...] = total[...].astype(jnp.bfloat16)


def outer(tokens, rstd, gain, d_qkv):
    rows = lambda n: pl.BlockSpec((256, n), lambda s: (s, 0))
    return pl.pallas_call(
        outer_kernel,
        grid=(4,),
        in_specs=[rows(D), rows(1), pl.BlockSpec((1, D), lambda s: (0, 0)), rows(768)],
        out_specs=pl.BlockSpec((D, 768), lambda s: (0, 0)),
        out_shape=jax.ShapeDtypeStruct((D, 768), jnp.bfloat16),
        scratch_shapes=[pltpu.VMEM((D, 768), jnp.float32)],
        compiler_params=pltpu.CompilerParams(vmem_limit_bytes=VMEM_LIMIT),
        cost_estimate=pl.CostEstimate(
            flops=2 * 1024 * D * 768, bytes_accessed=16 << 20, transcendentals=0
        ),
    )(tokens, rstd, gain, d_qkv)


def attend_kernel(
    q_pre, k_pre, v_pre, rstd_q, rstd_k, gain_q, gain_k, cosine, sine,
    attended, q_out, k_out, v_out, total, v_t,
):
    i = pl.program_id(1)

    @pl.when(i == 0)
    def _():
        cos, sin = cosine[...], sine[...]
        q_out[0] = roped(q_pre[...] * rstd_q[...] * gain_q[0], cos, sin).astype(jnp.bfloat16)
        k_out[0] = roped(k_pre[...] * rstd_k[...] * gain_k[0], cos, sin).astype(jnp.bfloat16)
        v_out[0] = v_pre[...].astype(jnp.bfloat16)
        v_t[...] = jnp.transpose(v_pre[...]).astype(jnp.bfloat16)

    query = q_out[0, pl.ds(pl.multiple_of(i * SPAN, SPAN), SPAN), :]
    scores = dot_t(k_out[0], query) * SCALE
    most = jnp.max(scores, axis=0, keepdims=True)
    weights = jnp.exp(scores - most)
    mass = jnp.sum(weights, axis=0, keepdims=True)
    total[0] = most + jnp.log(mass)
    probs = (weights / mass).astype(jnp.bfloat16)
    attended[0] = jnp.transpose(dot(v_t[...], probs)).astype(jnp.bfloat16)


SPAN = 256


def attend(qkv, rstd_q, rstd_k, gain_q, gain_k, cosine, sine):
    column = pl.BlockSpec((1024, 1), lambda h, i: (0, 0))
    gain = pl.BlockSpec((1, 1, 128), lambda h, i: (h, 0, 0))
    table = pl.BlockSpec((1024, 128), lambda h, i: (0, 0))
    head = pl.BlockSpec((1, 1024, 128), lambda h, i: (h, 0, 0))
    head_shape = jax.ShapeDtypeStruct((2, 1024, 128), jnp.bfloat16)
    return pl.pallas_call(
        attend_kernel,
        grid=(2, 1024 // SPAN),
        in_specs=[
            pl.BlockSpec((1024, 128), lambda h, i: (0, h)),
            pl.BlockSpec((1024, 128), lambda h, i: (0, 2 + h)),
            pl.BlockSpec((1024, 128), lambda h, i: (0, 4 + h)),
            column,
            column,
            gain,
            gain,
            table,
            table,
        ],
        out_specs=[
            pl.BlockSpec((1, SPAN, 128), lambda h, i: (i, 0, h)),
            head,
            head,
            head,
            pl.BlockSpec((1, 1, SPAN), lambda h, i: (h, 0, i)),
        ],
        out_shape=[
            jax.ShapeDtypeStruct((1024 // SPAN, SPAN, 256), jnp.bfloat16),
            head_shape,
            head_shape,
            head_shape,
            jax.ShapeDtypeStruct((2, 1, 1024), jnp.float32),
        ],
        scratch_shapes=[pltpu.VMEM((128, 1024), jnp.bfloat16)],
        compiler_params=pltpu.CompilerParams(vmem_limit_bytes=VMEM_LIMIT),
        cost_estimate=pl.CostEstimate(
            flops=2 * 4 * 1024 * 1024 * 128, bytes_accessed=8 << 20, transcendentals=2 << 20
        ),
    )(
        qkv,
        qkv,
        qkv,
        rstd_q,
        rstd_k,
        gain_q.reshape(2, 1, 128),
        gain_k.reshape(2, 1, 128),
        cosine,
        sine,
    )


def attend_back_kernel(
    d_att, q, k, v, total, cosine, sine, d_q, d_k, d_v, k_t, k_acc, v_acc
):
    i = pl.program_id(1)

    @pl.when(i == 0)
    def _():
        k_t[...] = jnp.transpose(k[0].astype(jnp.float32)).astype(jnp.bfloat16)
        k_acc[...] = jnp.zeros_like(k_acc)
        v_acc[...] = jnp.zeros_like(v_acc)

    at = pl.ds(pl.multiple_of(i * SPAN, SPAN), SPAN)
    query = q[0, at, :]
    probs = jnp.exp(dot_t(k[0], query) * SCALE - total[0])
    d_probs = dot_t(v[0], d_att[...])
    spread = jnp.sum(probs * d_probs, axis=0, keepdims=True)
    d_scores = (probs * (d_probs - spread)).astype(jnp.bfloat16)
    v_acc[...] += dot(probs.astype(jnp.bfloat16), d_att[...])
    k_acc[...] += dot(d_scores, query)
    d_query = jnp.transpose(dot(k_t[...], d_scores)) * SCALE
    d_q[...] = roped(d_query, cosine[at, :], -sine[at, :])

    @pl.when(i == pl.num_programs(1) - 1)
    def _():
        d_k[...] = roped(k_acc[...] * SCALE, cosine[...], -sine[...])
        d_v[...] = v_acc[...].reshape(4, 256, 128).astype(jnp.bfloat16)


def attend_back(d_att, q, k, v, total, cosine, sine):
    table = pl.BlockSpec((1024, 128), lambda h, i: (0, 0))
    head = pl.BlockSpec((1, 1024, 128), lambda h, i: (h, 0, 0))
    columns = pl.BlockSpec((1024, 128), lambda h, i: (0, h))
    tile = pl.BlockSpec((SPAN, 128), lambda h, i: (i, h))
    return pl.pallas_call(
        attend_back_kernel,
        grid=(2, 1024 // SPAN),
        in_specs=[
            tile,
            head,
            head,
            head,
            pl.BlockSpec((1, 1, SPAN), lambda h, i: (h, 0, i)),
            table,
            table,
        ],
        out_specs=[tile, columns, pl.BlockSpec((4, 256, 128), lambda h, i: (0, 0, h))],
        out_shape=[
            jax.ShapeDtypeStruct((1024, 256), jnp.float32),
            jax.ShapeDtypeStruct((1024, 256), jnp.float32),
            jax.ShapeDtypeStruct((4, 256, 256), jnp.bfloat16),
        ],
        scratch_shapes=[
            pltpu.VMEM((128, 1024), jnp.bfloat16),
            pltpu.VMEM((1024, 128), jnp.float32),
            pltpu.VMEM((1024, 128), jnp.float32),
        ],
        compiler_params=pltpu.CompilerParams(vmem_limit_bytes=VMEM_LIMIT),
        cost_estimate=pl.CostEstimate(
            flops=2 * 10 * 1024 * 1024 * 128, bytes_accessed=8 << 20, transcendentals=2 << 20
        ),
    )(d_att, q, k, v, total, cosine, sine)


CHUNKS = 2
PART = FF // CHUNKS
WIDE = 3 * PART
VMEM_LIMIT = 58 * 1024 * 1024


def pack_kernel(gate_up, down, out):
    down_t = jnp.transpose(down[0].astype(jnp.float32)).astype(jnp.bfloat16)
    for f in range(CHUNKS):
        out[0, :, pl.ds(f * WIDE, PART)] = gate_up[0, :, pl.ds(f * PART, PART)]
        out[0, :, pl.ds(f * WIDE + PART, PART)] = gate_up[0, :, pl.ds(FF + f * PART, PART)]
        out[0, :, pl.ds(f * WIDE + 2 * PART, PART)] = down_t[:, f * PART : (f + 1) * PART]


def pack_experts(gate_up, down):
    return pl.pallas_call(
        pack_kernel,
        grid=(2,),
        in_specs=[
            pl.BlockSpec((1, 128, 2 * FF), lambda m: (m, 0, 0)),
            pl.BlockSpec((1, FF, 128), lambda m: (m, 0, 0)),
        ],
        out_specs=pl.BlockSpec((1, 128, 3 * FF), lambda m: (m, 0, 0)),
        out_shape=jax.ShapeDtypeStruct((2, 128, 3 * FF), jnp.bfloat16),
        compiler_params=pltpu.CompilerParams(vmem_limit_bytes=VMEM_LIMIT),
        cost_estimate=pl.CostEstimate(flops=0, bytes_accessed=4 << 20, transcendentals=0),
    )(gate_up, down)


def unpack_kernel(first, second, gate_up, down):
    for m, part in enumerate((first, second)):

        @pl.when(pl.program_id(0) == m)
        def _():
            for f in range(CHUNKS):
                at = f * WIDE
                gate_up[0, :, pl.ds(f * PART, PART)] = part[:, pl.ds(at, PART)].astype(jnp.float32)
                up = part[:, pl.ds(at + PART, PART)].astype(jnp.float32)
                gate_up[0, :, pl.ds(FF + f * PART, PART)] = up
                down_t = part[:, pl.ds(at + 2 * PART, PART)].astype(jnp.float32)
                down[0, pl.ds(f * PART, PART), :] = jnp.transpose(down_t)


def unpack_experts(first, second):
    whole = pl.BlockSpec((128, 3 * FF), lambda m: (0, 0))
    return pl.pallas_call(
        unpack_kernel,
        grid=(2,),
        in_specs=[whole, whole],
        out_specs=[
            pl.BlockSpec((1, 128, 2 * FF), lambda m: (m, 0, 0)),
            pl.BlockSpec((1, FF, 128), lambda m: (m, 0, 0)),
        ],
        out_shape=[
            jax.ShapeDtypeStruct((2, 128, 2 * FF), jnp.float32),
            jax.ShapeDtypeStruct((2, FF, 128), jnp.float32),
        ],
        compiler_params=pltpu.CompilerParams(vmem_limit_bytes=VMEM_LIMIT),
        cost_estimate=pl.CostEstimate(flops=0, bytes_accessed=4 << 20, transcendentals=0),
    )(first, second)


def turned(a):
    return jnp.transpose(a.astype(jnp.float32)).astype(jnp.bfloat16)


def open_kernel(
    seat, gate, normed, cot, weights,
    part, rows_t, d_out_t, cot_rows, pick_t, weight, rows, d_out,
):
    @pl.when(pl.program_id(1) == 0)
    def _():
        taken = lax.broadcasted_iota(jnp.int32, (CAP, 1024), 0) == seat[0]
        slot_weight = jnp.sum(jnp.where(taken, gate[0], 0.0), axis=1, keepdims=True)
        weight[0] = slot_weight
        pick = jnp.where(taken, 1.0, 0.0)
        pick_t[0] = turned(pick)
        pick = pick.astype(jnp.bfloat16)
        for at in range(0, HALF, 512):
            spot = pl.ds(at, 512)
            found = dot(pick, normed[:, spot])
            rows[:, spot] = found.astype(jnp.bfloat16)
            rows_t[0, spot, :] = turned(found)
            picked = dot(pick, cot[:, spot])
            cot_rows[0, :, spot] = picked.astype(jnp.bfloat16)
            picked = picked * slot_weight
            d_out[:, spot] = picked.astype(jnp.bfloat16)
            d_out_t[0, spot, :] = turned(picked)

    for k, left in enumerate((rows, rows, d_out)):
        at = pl.ds(k * PART, PART)
        part[0, :, at] = dot(left[...], weights[0, :, at]).astype(jnp.bfloat16)


def open_experts(seat, gate, normed, cot, weights):
    whole = pl.BlockSpec((1024, HALF), lambda h, f: (0, 0))
    line = pl.BlockSpec((1, 1, 1024), lambda h, f: (h, 0, 0))
    slot = pl.BlockSpec((1, CAP, HALF), lambda h, f: (h, 0, 0))
    slot_t = pl.BlockSpec((1, HALF, CAP), lambda h, f: (h, 0, 0))
    shape_t = jax.ShapeDtypeStruct((2, HALF, CAP), jnp.bfloat16)
    return pl.pallas_call(
        open_kernel,
        grid=(2, CHUNKS),
        in_specs=[
            line,
            line,
            whole,
            whole,
            pl.BlockSpec((1, HALF, WIDE), lambda h, f: (h, 0, f)),
        ],
        out_specs=[
            pl.BlockSpec((1, CAP, WIDE), lambda h, f: (h, 0, f)),
            slot_t,
            slot_t,
            slot,
            slot_t,
            pl.BlockSpec((1, CAP, 1), lambda h, f: (h, 0, 0)),
        ],
        out_shape=[
            jax.ShapeDtypeStruct((2, CAP, 3 * FF), jnp.bfloat16),
            shape_t,
            shape_t,
            jax.ShapeDtypeStruct((2, CAP, HALF), jnp.bfloat16),
            shape_t,
            jax.ShapeDtypeStruct((2, CAP, 1), jnp.float32),
        ],
        scratch_shapes=[pltpu.VMEM((CAP, HALF), jnp.bfloat16)] * 2,
        compiler_params=pltpu.CompilerParams(vmem_limit_bytes=VMEM_LIMIT),
        cost_estimate=pl.CostEstimate(
            flops=2 * 2 * CAP * 1024 * 5120, bytes_accessed=30 << 20, transcendentals=0
        ),
    )(seat, gate, normed, cot, weights)


def close_kernel(
    first, seat, own, received, rows_t, d_out_t, cot_rows, pick_t, weight, weights, *refs
):
    if first:
        moe, d_normed, grads, d_token, moe_acc, d_acc, out_acc, row_acc = refs
    else:
        moe_in, d_in, moe, d_normed, grads, d_token, moe_acc, d_acc, out_acc, row_acc = refs
    h, f = pl.program_id(0), pl.program_id(1)

    @pl.when((h == 0) & (f == 0))
    def _():
        if first:
            moe_acc[...] = jnp.zeros_like(moe_acc)
            d_acc[...] = jnp.zeros_like(d_acc)
        else:
            for s in range(4):
                moe_acc[pl.ds(s * 256, 256), :] = moe_in[s].astype(jnp.float32)
                d_acc[pl.ds(s * 256, 256), :] = d_in[s].astype(jnp.float32)

    @pl.when(f == 0)
    def _():
        out_acc[...] = jnp.zeros_like(out_acc)
        row_acc[...] = jnp.zeros_like(row_acc)

    def both(k):
        at = pl.ds(k * PART, PART)
        return own[0, :, at].astype(jnp.float32) + received[0, :, at].astype(jnp.float32)

    gate, up, d_hidden = both(0), both(1), both(2)
    sig = jax.nn.sigmoid(gate)
    scaled = gate * sig
    hidden = (scaled * up).astype(jnp.bfloat16)
    d_gate = (d_hidden * up * sig * (1.0 + gate * (1.0 - sig))).astype(jnp.bfloat16)
    d_up = (d_hidden * scaled).astype(jnp.bfloat16)
    out_acc[...] += dot_t(hidden, weights[0, :, pl.ds(2 * PART, PART)])
    row_acc[...] += dot_t(d_gate, weights[0, :, pl.ds(0, PART)])
    row_acc[...] += dot_t(d_up, weights[0, :, pl.ds(PART, PART)])
    grads[0, :, pl.ds(0, PART)] = dot(rows_t[0], d_gate).astype(jnp.bfloat16)
    grads[0, :, pl.ds(PART, PART)] = dot(rows_t[0], d_up).astype(jnp.bfloat16)
    grads[0, :, pl.ds(2 * PART, PART)] = dot(d_out_t[0], hidden).astype(jnp.bfloat16)

    @pl.when(f == CHUNKS - 1)
    def _():
        d_weight = jnp.sum(out_acc[...] * cot_rows[0].astype(jnp.float32), axis=1, keepdims=True)
        taken = lax.broadcasted_iota(jnp.int32, (CAP, 1024), 0) == seat[0]
        d_token[0] = jnp.sum(jnp.where(taken, d_weight, 0.0), axis=0, keepdims=True)
        weighted = (weight[0] * out_acc[...]).astype(jnp.bfloat16)
        d_rows = row_acc[...].astype(jnp.bfloat16)
        for at in range(0, HALF, 512):
            spot = pl.ds(at, 512)
            moe_acc[:, spot] += dot(pick_t[0], weighted[:, at : at + 512])
            d_acc[:, spot] += dot(pick_t[0], d_rows[:, at : at + 512])

    @pl.when((h == 1) & (f == CHUNKS - 1))
    def _():
        for s in range(4):
            moe[s] = moe_acc[pl.ds(s * 256, 256), :].astype(moe.dtype)
            d_normed[s] = d_acc[pl.ds(s * 256, 256), :].astype(d_normed.dtype)


def close_experts(seat, own, received, state, weights, before):
    whole = pl.BlockSpec((4, 256, HALF), lambda h, f: (0, 0, 0))
    line = pl.BlockSpec((1, 1, 1024), lambda h, f: (h, 0, 0))
    slot = pl.BlockSpec((1, CAP, HALF), lambda h, f: (h, 0, 0))
    slot_t = pl.BlockSpec((1, HALF, CAP), lambda h, f: (h, 0, 0))
    part = pl.BlockSpec((1, CAP, WIDE), lambda h, f: (h, 0, f))
    wide = pl.BlockSpec((1, HALF, WIDE), lambda h, f: (h, 0, f))
    full = jax.ShapeDtypeStruct((4, 256, HALF), jnp.bfloat16)

    def body(*refs):
        close_kernel(not before, *refs)

    return pl.pallas_call(
        body,
        grid=(2, CHUNKS),
        in_specs=[
            line,
            part,
            part,
            slot_t,
            slot_t,
            slot,
            slot_t,
            pl.BlockSpec((1, CAP, 1), lambda h, f: (h, 0, 0)),
            wide,
        ]
        + [whole] * len(before),
        out_specs=[whole, whole, wide, line],
        out_shape=[
            full,
            full,
            jax.ShapeDtypeStruct((2, HALF, 3 * FF), jnp.bfloat16),
            jax.ShapeDtypeStruct((2, 1, 1024), jnp.float32),
        ],
        scratch_shapes=[
            pltpu.VMEM((1024, HALF), jnp.float32),
            pltpu.VMEM((1024, HALF), jnp.float32),
            pltpu.VMEM((CAP, HALF), jnp.float32),
            pltpu.VMEM((CAP, HALF), jnp.float32),
        ],
        compiler_params=pltpu.CompilerParams(vmem_limit_bytes=VMEM_LIMIT),
        cost_estimate=pl.CostEstimate(
            flops=2 * 2 * CAP * 1024 * 8192, bytes_accessed=50 << 20, transcendentals=2 * CAP * FF
        ),
    )(seat, own, received, *state, weights, *before)


def on_device(
    tokens,
    cotangent,
    w_qkv,
    w_out,
    w_router,
    norm_attn,
    norm_moe,
    query_gain,
    key_gain,
    w_gate_up,
    w_down,
    routes,
    block_order,
):
    y, zh, c = lax.axis_index("y"), lax.axis_index("zh"), lax.axis_index("c")
    plane = ("zh", "zl", "x")
    own_first = c == 0

    low, high = split_halves(tokens[0])
    low, high, w_qkv = lax.optimization_barrier((low, high, w_qkv))
    x_blocks = jnp.concatenate(to_half(low, high, zh, c))
    x_blocks, block_order, w_gate_up, cotangent, routes = lax.optimization_barrier(
        (x_blocks, block_order, w_gate_up, cotangent, routes)
    )
    x_own = y_gather(x_blocks)
    x_par = [other_core(part) for part in x_own]
    place = jnp.full((8, 128), block_order[0, 0], jnp.int32).astype(jnp.float32)
    places = y_gather(jnp.stack(to_half(place, place, zh, c)))
    places = jnp.stack(places)[:, :, 0, 0].reshape(8)

    pieces = w_qkv.reshape(16, 3, 8, 256).transpose(2, 0, 1, 3).reshape(8, 16, 768)
    small = jnp.concatenate(
        [norm_attn[:, None], norm_moe[:, None], w_router, query_gain[:, None], key_gain[:, None]],
        axis=1,
    )
    small = jnp.pad(small, ((0, 0), (0, 108)))
    pieces = jnp.concatenate([pieces, jnp.broadcast_to(small, (8, 16, 128))], axis=2)
    pieces = trade(pieces, y, c).reshape(128, 896)
    out_low, out_high = split_halves(w_out)
    out_par = other_core(jnp.where(own_first, out_high, out_low))
    out_own = jnp.where(own_first, out_low, out_high)
    out_both = jnp.where(
        own_first, jnp.concatenate([out_own, out_par]), jnp.concatenate([out_par, out_own])
    )
    out_both = out_both.reshape(32, 4, 256).transpose(1, 0, 2).reshape(128, 256)
    dense = jnp.concatenate([pieces, out_both], axis=1)
    dense, w_gate_up = lax.optimization_barrier((dense, w_gate_up))
    dense = lax.all_gather(dense, plane, axis=0, tiled=True).reshape(2, 2, 4, 4, 2, 16, 1152)

    expert_w = [
        lax.all_gather(part, plane, axis=0, tiled=True).reshape(2, HALF, 3 * FF)
        for part in pack_experts(w_gate_up, w_down)
    ]

    cot_low, cot_high = split_halves(cotangent[0])
    cot_here = jnp.concatenate(to_half(cot_low, cot_high, zh, c))
    cot_sent, x_own = lax.optimization_barrier((cot_here, x_own))
    cot_parts = y_gather(cot_sent)
    route_t = routes[0].T
    route_t = jnp.where(c == zh, route_t, other_core(route_t))
    route_t = by_distance(route_t.reshape(4, 4, 256), y).reshape(4, 1024)

    def rolled(a):
        a = a.transpose(1, 3, 0, 2, 4, 5, 6).reshape(2, HALF, -1)
        return jnp.where(own_first, a, a[::-1])

    qkv_w = rolled(dense[..., :768]).reshape(D, 768)
    small_all = dense[..., 768:788]
    small_rolled = f32(rolled(small_all))
    gain_attn = small_rolled[:, :, 0]
    gain_moe = small_rolled[0, :, 1]
    router_w = bf16(small_rolled[0, :, 2:18])
    small_true = f32(small_all[..., 18:20].transpose(3, 0, 1, 2, 4, 5, 6).reshape(8, 256, 2))
    head_block = y * 2 + c
    mine = lax.dynamic_index_in_dim(small_true, head_block, 0, keepdims=False)
    gain_query, gain_key = mine[:, 0], mine[:, 1]
    out_w = dense.reshape(16, 128, 1152)[:, :, 896:].reshape(16, 4, 32, 256)
    out_w = out_w.transpose(0, 2, 1, 3).reshape(2, 256, HALF)
    out_w = jnp.where(own_first, out_w, out_w[::-1]).reshape(512, HALF)

    qkv, x_all, rstd_one, squares = project(x_own, x_par, gain_attn, qkv_w)
    squares = squares.reshape(2, 8, 1024)[:, 0]
    rstd = lax.rsqrt(ring_sum(squares, y) / D + epsilon)
    rstd_q, rstd_k = rstd[0][:, None], rstd[1][:, None]
    here = places[:, None, None] == jnp.arange(8, dtype=jnp.float32)[None, :, None]
    block_cos, block_sin, row_cos, row_sin = angle_tables()
    block_cos = jnp.sum(jnp.where(here, block_cos, 0.0), axis=1)[:, None]
    block_sin = jnp.sum(jnp.where(here, block_sin, 0.0), axis=1)[:, None]
    cosine = block_cos * row_cos - block_sin * row_sin
    sine = block_sin * row_cos + block_cos * row_sin
    cosine = jnp.concatenate([cosine, cosine], axis=2).reshape(1024, 128)
    sine = jnp.concatenate([-sine, sine], axis=2).reshape(1024, 128)
    qkv, out_w, cosine, sine = lax.optimization_barrier((qkv, out_w, cosine, sine))
    attended, *heads = attend(qkv, rstd_q, rstd_k, gain_query, gain_key, cosine, sine)
    attended, cot_parts = lax.optimization_barrier(
        (attended.reshape(1024, 256), cot_parts)
    )
    cot_all = jnp.concatenate(cot_parts)
    attended = jnp.concatenate([attended, other_core(attended)], axis=1)
    out_parts, out_here = output_product(attended, out_w)
    got = [from_chip(out_parts[step], 4 - step) for step in (1, 2, 3)]
    x_here = f32(x_all[:256, :HALF])
    after, square = residual(x_all, out_here, got)

    square = square.reshape(256)
    rstd_two = lax.rsqrt((square + other_core(square)) / D + epsilon)[:, None]
    after_hat = after * rstd_two
    normed_two = bf16(after_hat * gain_moe)
    normed_all = jnp.concatenate(y_gather(normed_two))
    router_t = router_w.T
    logits = logits_of(router_t, normed_all)
    logits = logits + other_core(logits)
    picked = route_t[:, None, :] == jnp.arange(16, dtype=jnp.int32)[None, :, None]
    routed = jnp.sum(jnp.where(picked, logits[None], 0.0), axis=1)
    routed = jnp.exp(routed - jnp.max(routed, axis=0, keepdims=True))
    gates = routed / (routed[0] + routed[1] + routed[2] + routed[3])

    before, d_gates, expert_grads = (), jnp.zeros((4, 1024), jnp.float32), []
    for m in range(2):
        chosen = route_t[None] == y * 4 + jnp.arange(2, dtype=jnp.int32)[:, None, None] * 2 + m
        hit = jnp.sum(chosen.astype(jnp.int32), axis=1)
        rank = jnp.cumsum(hit, axis=1) - hit
        seat = jnp.where(hit > 0, rank, CAP)[:, None]
        gate_token = jnp.sum(jnp.where(chosen, gates[None], 0.0), axis=1)[:, None]
        seat, before = lax.optimization_barrier((seat, before))
        part, *state = open_experts(seat, gate_token, normed_all, cot_all, expert_w[m])
        moe_sum, d_normed, grads, d_token = close_experts(
            seat, part, other_core(part), state, expert_w[m], before
        )
        before = (moe_sum, d_normed)
        d_gates = d_gates + jnp.sum(jnp.where(chosen, d_token, 0.0), axis=0)
        expert_grads.append(
            lax.psum_scatter(grads.reshape(D, 3 * FF), plane, scatter_dimension=0, tiled=True)
        )

    def ring_scatter(a):
        a = a.reshape(4, 256, HALF)
        return sum(f32(g) for g in y_scatter([a[s] for s in range(4)]))

    d_got = y_scatter([d_normed[step] for step in range(4)])
    d_gates = d_gates.reshape(4, 4, 256)
    d_gates = sum(y_scatter([d_gates[:, s] for s in range(4)]))
    d_gates = d_gates + other_core(d_gates)

    gates_here, picked_here = gates[:, :256], picked[:, :, :256]
    shared = gates_here * d_gates
    shared = shared[0] + shared[1] + shared[2] + shared[3]
    d_routed = gates_here * (d_gates - shared)
    d_logits = jnp.sum(jnp.where(picked_here, d_routed[:, None, :], 0.0), axis=0)
    grad_router, d_normed_here, grad_norm_moe, along = route_back(
        normed_two, d_logits, router_t, after, rstd_two, gain_moe[None], d_got
    )
    grad_router, grad_norm_moe = grad_router.T, grad_norm_moe.reshape(HALF)
    d_scaled = d_normed_here * gain_moe
    along = along.reshape(256)
    along = (along + other_core(along))[:, None] / D
    d_after = f32(cot_here) + rstd_two * (d_scaled - after_hat * along)

    d_attn = jnp.concatenate(y_gather(bf16(d_after)))
    moe_sum, d_attn = lax.optimization_barrier((moe_sum, d_attn))
    moe_here = ring_scatter(moe_sum)
    d_att, d_other = heads_product(d_attn, out_w)
    d_att = bf16(d_att + other_core(d_other))
    d_att, expert_grads[0] = lax.optimization_barrier((d_att, expert_grads[0]))
    d_query, d_key, d_value = attend_back(d_att, *heads, cosine, sine)
    d_query, d_attn = lax.optimization_barrier((d_query, d_attn))
    grad_out = out_grad(attended, d_attn)
    along, grad_query_gain, grad_key_gain = along_sums(
        d_query, d_key, qkv, rstd_q, rstd_k, gain_query, gain_key
    )
    grad_query_gain, grad_key_gain = grad_query_gain.reshape(256), grad_key_gain.reshape(256)
    along = ring_sum(along.reshape(2, 8, 1024)[:, 0], y)[:, :, None] / D
    along, moe_here = lax.optimization_barrier((along, moe_here))
    d_qkv, d_par, d_own, grad_norm_attn = spread(
        d_query, d_key, d_value, qkv, rstd_q, rstd_k, along[0], along[1],
        gain_query, gain_key, x_all, rstd_one, qkv_w,
    )
    grad_norm_attn = grad_norm_attn.reshape(D)
    received = other_core(d_par)
    received, d_qkv = lax.optimization_barrier((received, d_qkv))
    d_sent = bf16(d_own + f32(received))
    got = y_scatter([d_sent[s * 256 : s * 256 + 256] for s in range(4)])
    grad_qkv = outer(x_all, rstd_one, gain_attn.reshape(1, D), d_qkv)
    got, moe_here = lax.optimization_barrier((got, moe_here))
    layer_output = from_half(bf16(after + moe_here), zh, c)[None]
    hat_here = x_here * rstd_one[:256]
    d_normed_one, along = back_sums(x_all, rstd_one, gain_attn[:1], got)
    along = along.reshape(256)
    along = (along + other_core(along))[:, None] / D
    grad_tokens = bf16(d_after + rstd_one[:256] * (d_normed_one - hat_here * along))

    wide = jnp.concatenate([grad_norm_moe[:, None], grad_router], axis=1)
    wide = jnp.pad(wide, ((0, HALF), (0, 0)))
    extras = jnp.concatenate([grad_norm_attn[:, None], wide], axis=1).reshape(2, HALF, 18)
    extras = jnp.where(own_first, extras, extras[::-1]).reshape(2, 4, 2, 4, 2, 16, 18)
    gains = jnp.stack([grad_query_gain, grad_key_gain], axis=1)
    at_home = jnp.arange(8)[:, None, None] == head_block
    gains = jnp.where(at_home, gains[None], 0.0).reshape(4, 2, 2, 4, 2, 16, 2)
    extras = jnp.concatenate(
        [extras.transpose(2, 0, 3, 1, 4, 5, 6), gains.transpose(1, 2, 3, 0, 4, 5, 6)], axis=-1
    )
    coarse = bf16(extras)
    extras = jnp.concatenate([coarse, bf16(extras - f32(coarse))], axis=-1)
    extras = jnp.pad(extras, ((0, 0),) * 6 + ((0, 88),))
    both = grad_qkv.reshape(2, HALF, 768)
    both = jnp.where(own_first, both, both[::-1]).reshape(2, 4, 2, 4, 2, 16, 768)
    both = both.transpose(2, 0, 3, 1, 4, 5, 6)
    both = jnp.concatenate([both, extras], axis=-1).reshape(16, 128, 896)
    grad_out = grad_out.reshape(2, 256, HALF)
    grad_out = jnp.where(own_first, grad_out, grad_out[::-1]).reshape(16, 32, 4, 256)
    grad_out = grad_out.transpose(0, 2, 1, 3).reshape(16, 128, 256)
    both = jnp.concatenate([both, grad_out], axis=2).reshape(D, 1152)
    both, expert_grads, got = lax.optimization_barrier((both, expert_grads, got))
    both = lax.psum_scatter(both, plane, scatter_dimension=0, tiled=True)
    grad_out = both[:, 896:].reshape(4, 32, 256).transpose(1, 0, 2).reshape(32, HALF)
    both = f32(trade(both[:, :896].reshape(8, 16, 896), y, c))
    grad_w_qkv = both[:, :, :768].reshape(8, 16, 3, 256).transpose(1, 2, 0, 3).reshape(16, 3 * D)
    smalls = jnp.sum(both[:, :, 768:788] + both[:, :, 788:808], axis=0)

    out_own = jnp.where(own_first, grad_out[:16], grad_out[16:])
    out_par = other_core(jnp.where(own_first, grad_out[16:], grad_out[:16]))
    grad_w_out = jnp.where(own_first, join_halves(out_own, out_par), join_halves(out_par, out_own))
    grad_w_out = f32(grad_w_out)

    grad_gate_up, grad_down = unpack_experts(*expert_grads)
    return (
        layer_output,
        from_half(grad_tokens, zh, c)[None],
        grad_w_qkv,
        grad_w_out,
        smalls[:, 2:18],
        smalls[:, 0],
        smalls[:, 1],
        smalls[:, 18],
        smalls[:, 19],
        grad_gate_up,
        grad_down,
    )


def solution(mesh):
    fine = Mesh(mesh.devices.reshape(4, 2, 2, 4, 2), ("y", "zh", "zl", "x", "c"))
    ctx, fsdp = ("y", "zh"), ("zl", "x", "c")
    rows, blocks, line = P(ctx + fsdp, None), P(fsdp, ctx, None), P(ctx + fsdp)
    gate_up, down = P(ctx, fsdp, None), P(ctx, None, fsdp)
    return jax.shard_map(
        on_device,
        mesh=fine,
        in_specs=(blocks, blocks, rows, rows, rows, line, line, line, line, gate_up, down)
        + (P(fsdp, None, None), P(fsdp, ctx)),
        out_specs=(blocks, blocks, rows, rows, rows, line, line, line, line, gate_up, down),
        check_vma=False,
    )
```

time: 689 us -> 647 us (0.939)
  Pallas kernels: 0 us -> 183 us
  matrix products: 159 us -> 0 us
  other arithmetic: 76.4 us -> 47.2 us
  waiting for transfers between devices: 275 us -> 250 us
    pallas_call x0 -> x19, Pallas kernels: none -> 183 us  [the longest x2 55.1 us: close_experts(): pl.pallas_call(body, grid=(2, CHUNKS), in_specs=[line, part, part, slot_t...]
    dot_general x31 -> x0, matrix products: 154 us -> none  [the longest x14 99.6 us: per_expert(): return jnp.einsum(pattern, a, b, preferred_element_type=jnp.float32)]
    all_gather x2, waiting for transfers between devices: 31.2 us -> 0.01 us  [on_device(): lax.all_gather(part, plane, axis=0, tiled=True).reshape(2, HALF, 3 * FF)]
    ppermute x26, waiting for transfers between devices: 6.22 us -> 26 us  [other_core(): return lax.ppermute(a, 'c', [(0, 1), (1, 0)])]
    reduce_scatter x1, waiting for transfers between devices: 66.3 us -> 51.4 us  [on_device(): both = lax.psum_scatter(both, plane, scatter_dimension=0, tiled=True)]
    convert_element_type x13 -> x8, other arithmetic: 21.5 us -> 9.56 us  [bf16(): return a.astype(jnp.bfloat16)]
    add x3, other arithmetic: 10.4 us -> 0.03 us  [the longest x1 0.01 us: on_device(): gates = routed / (routed[0] + routed[1] + routed[2] + routed[3])]
    concatenate x11 -> x2, other arithmetic: 13.3 us -> 2.88 us  [the longest x1 1.49 us: on_device(): normed_all = jnp.concatenate(y_gather(normed_two))]
  transfers between devices with their start and end apart: 79 -> 79, of which waited for: 37 -> 45; matrix products, arithmetic and copies ran while one was open for 35% -> 15% of each run, Pallas kernels for 0% -> 29%
where the time goes in v1:
time: 647 us; the launch traced here: 636 us
  waiting for transfers between devices  250 us (39%)
  Pallas kernels  183 us (28%)
  starting transfers between devices  74.9 us (12%)
  local copies, waits for them, and re-layouts  65 us (10%)
  other arithmetic  47.2 us (7%)
  between operations  16.7 us (3%)
    ppermute x42, waiting for transfers between devices, from_chip(): return lax.ppermute(a, 'y', [(i, (i + step) % 4) for i in range(4)])  149 us
    ppermute x42, starting transfers between devices, from_chip(): return lax.ppermute(a, 'y', [(i, (i + step) % 4) for i in range(4)])  56.2 us
    pallas_call x2, Pallas kernels, close_experts(): pl.pallas_call(body, grid=(2, CHUNKS), in_specs=[line, part, part, slot_t...  55.1 us
    reduce_scatter x1, waiting for transfers between devices, on_device(): both = lax.psum_scatter(both, plane, scatter_dimension=0, tiled=True)  51.4 us
    pallas_call x2, Pallas kernels, open_experts(): pl.pallas_call(open_kernel, grid=(2, CHUNKS), in_specs=[line, line, whole...  33.6 us
    ppermute x26, waiting for transfers between devices, other_core(): return lax.ppermute(a, 'c', [(0, 1), (1, 0)])  26 us
    ppermute x5, waiting for transfers between devices, other_layer(): return lax.ppermute(a, 'zh', [(0, 1), (1, 0)])  22.7 us
    unnamed x172, local copies, waits for them, and re-layouts  20.7 us
  transfers between devices with their start and end apart: 79, of which 45 were waited for; matrix products, arithmetic and copies ran while one was open for 15% of the time, Pallas kernels for 29%

profile of v1, /device:TPU:32, one launch (start us, length us, event | category | flops | bytes accessed | tf_op | source)
XLA Modules:
  0.0 636.1 jit_solution(9246708840319161467)
XLA Ops:
  30.8 4.5 collective-permute-done.1
  49.5 3.6 collective-permute-start.19
  70.5 19.4 %collective-permute-done.4.refs_1_ = bf16[256,1024]{1,0:T(8,128)(2,1)} collective-permute-done((bf16[256,1024]{1,0:T(8,128)(2,1)}, bf16[256,1024]{1,0:T(8,128)(2,1)}, u32[]{:S(2)}, u32[]{:S(2)}) %collective-permute-start.4) | collective-permute-done | bytes 524320 | tf_op jit(solution)/shard_map/ppermute | solution.py:46
  109.1 10.1 %shard_map.248 = (f32[1024,768]{1,0:T(8,128)}, bf16[1024,2048]{1,0:T(8,128)(2,1)}, f32[1024,1]{1,0:T(8,128)}, f32[16,1024]{1,0:T(8,128)}) custom-call(bf16[256,1024]{1,0:T(8,128)(2,1)} %pad_maximum_fusion.5.refs_0_, bf16[256,1024]{1,0:T(8,128)(2,1)} %collective-permute-done.4.refs_1_, bf16[256,1024]{1,0:T(8,128)(2,1)} %collective-permute-done.5.refs_2_, ...), custom_call_target="tpu_custom_call" | custom-call | flops 3221225472 | bytes 20971520 | tf_op jit(solution)/shard_map/pallas_call | solution.py:164
  136.2 13.2 %shard_map.249 = (bf16[4,256,256]{2,1,0:T(8,128)(2,1)}, bf16[2,1024,128]{2,1,0:T(8,128)(2,1)}, bf16[2,1024,128]{2,1,0:T(8,128)(2,1)}, bf16[2,1024,128]{2,1,0:T(8,128)(2,1)}, f32[2,1,1024]{2,1,0:T(1,128)}) custom-call(f32[1024,768]{1,0:T(8,128)} %get-tuple-element.123.q_pre.k_pre.v_pre, f32[1024,768]{1,0:T(8,128)} %get-tuple-element.123.q_pre.k_pre.v_pre, ...), custom_call_target="tpu_custom_call" | custom-call | flops 1073741824 | bytes 8388608 | tf_op jit(solution)/shard_map/pallas_call | solution.py:539
  153.6 5.2 shard_map.250
  164.1 11.2 %collective-permute-done.29.first = bf16[256,1024]{1,0:T(8,128)(2,1)} collective-permute-done((bf16[256,1024]{1,0:T(8,128)(2,1)S(1)}, bf16[256,1024]{1,0:T(8,128)(2,1)}, u32[]{:S(2)}, u32[]{:S(2)}) %collective-permute-start.29) | collective-permute-done | bytes 524320 | tf_op jit(solution)/shard_map/ppermute | solution.py:46
  178.2 10.1 %collective-permute-done.31.third = bf16[256,1024]{1,0:T(8,128)(2,1)} collective-permute-done((bf16[256,1024]{1,0:T(8,128)(2,1)S(1)}, bf16[256,1024]{1,0:T(8,128)(2,1)}, u32[]{:S(2)}, u32[]{:S(2)}) %collective-permute-start.31) | collective-permute-done | bytes 524320 | tf_op jit(solution)/shard_map/ppermute | solution.py:46
  202.6 19.7 %collective-permute-done.34 = bf16[256,1024]{1,0:T(8,128)(2,1)S(1)} collective-permute-done((bf16[256,1024]{1,0:T(8,128)(2,1)S(1)}, bf16[256,1024]{1,0:T(8,128)(2,1)S(1)}, u32[]{:S(2)}, u32[]{:S(2)}) %collective-permute-start.34) | collective-permute-done | bytes 524320 | tf_op jit(solution)/shard_map/ppermute | solution.py:46
  230.5 16.9 %shard_map.254 = (bf16[2,384,3072]{2,1,0:T(8,128)(2,1)}, bf16[2,1024,384]{2,1,0:T(8,128)(2,1)}, bf16[2,1024,384]{2,1,0:T(8,128)(2,1)}, bf16[2,384,1024]{2,1,0:T(...) custom-call(s32[2,1,1024]{2,1,0:T(1,128)} %compare_select_fusion.4.seat.refs_0_, ...), custom_call_target="tpu_custom_call" | custom-call | flops 8053063680 | bytes 31457280 | tf_op jit(solution)/shard_map/pallas_call | solution.py:748
  248.1 7.9 %collective-permute-done.38.refs_2_ = bf16[2,384,3072]{2,1,0:T(8,128)(2,1)} collective-permute-done((bf16[2,384,3072]{2,1,0:T(8,128)(2,1)}, bf16[2,384,3072]{2,1,0:T(8,128)(2,1)}, u32[]{:S(2)}, u32[]{:S(2)}) %collective-permute-start.38) | collective-permute-done | bytes 4718624 | tf_op jit(solution)/shard_map/ppermute | solution.py:42
  256.0 26.6 %shard_map.255 = (bf16[4,256,1024]{2,1,0:T(8,128)(2,1)}, bf16[4,256,1024]{2,1,0:T(8,128)(2,1)}, bf16[2,1024,3072]{2,1,0:T(8,128)(2,1)}, f32[2,1,1024]{2,1,0:T(1,128)}) custom-call(s32[2,1,1024]{2,1,0:T(1,128)} %compare_select_fusion.4.seat.refs_0_, bf16[2,384,3072]{2,1,0:T(8,128)(2,1)} %get-tuple-element.141.refs_1_, ...), custom_call_target="tpu_custom_call" | custom-call | flops 12884901888 | bytes 52428800 | tf_op jit(solution)/shard_map/pallas_call | solution.py:854
  284.9 16.6 %shard_map.256 = (bf16[2,384,3072]{2,1,0:T(8,128)(2,1)}, bf16[2,1024,384]{2,1,0:T(8,128)(2,1)}, bf16[2,1024,384]{2,1,0:T(8,128)(2,1)}, bf16[2,384,1024]{2,1,0:T(...) custom-call(s32[2,1,1024]{2,1,0:T(1,128)} %compare_select_fusion.5.seat.refs_0_, ...), custom_call_target="tpu_custom_call" | custom-call | flops 8053063680 | bytes 31457280 | tf_op jit(solution)/shard_map/pallas_call | solution.py:748
  302.3 7.9 %collective-permute-done.39.refs_2_ = bf16[2,384,3072]{2,1,0:T(8,128)(2,1)} collective-permute-done((bf16[2,384,3072]{2,1,0:T(8,128)(2,1)}, bf16[2,384,3072]{2,1,0:T(8,128)(2,1)}, u32[]{:S(2)}, u32[]{:S(2)}) %collective-permute-start.39) | collective-permute-done | bytes 4718624 | tf_op jit(solution)/shard_map/ppermute | solution.py:42
  310.1 28.5 %shard_map.257 = (bf16[4,256,1024]{2,1,0:T(8,128)(2,1)}, bf16[4,256,1024]{2,1,0:T(8,128)(2,1)}, bf16[2,1024,3072]{2,1,0:T(8,128)(2,1)}, f32[2,1,1024]{2,1,0:T(1,128)}) custom-call(s32[2,1,1024]{2,1,0:T(1,128)} %compare_select_fusion.5.seat.refs_0_, bf16[2,384,3072]{2,1,0:T(8,128)(2,1)} %get-tuple-element.150.refs_1_, ...), custom_call_target="tpu_custom_call" | custom-call | flops 12884901888 | bytes 52428800 | tf_op jit(solution)/shard_map/pallas_call | solution.py:854
  353.9 11.0 %collective-permute-done.44.refs_1_ = bf16[256,1024]{1,0:T(8,128)(2,1)S(1)} collective-permute-done((bf16[256,1024]{1,0:T(8,128)(2,1)S(1)}, bf16[256,1024]{1,0:T(8,128)(2,1)S(1)}, u32[]{:S(2)}, u32[]{:S(2)}) %collective-permute-start.44) | collective-permute-done | bytes 524320 | tf_op jit(solution)/shard_map/ppermute | solution.py:46
  367.2 10.5 %collective-permute-done.46.refs_3_ = bf16[256,1024]{1,0:T(8,128)(2,1)S(1)} collective-permute-done((bf16[256,1024]{1,0:T(8,128)(2,1)S(1)}, bf16[256,1024]{1,0:T(8,128)(2,1)S(1)}, u32[]{:S(2)}, u32[]{:S(2)}) %collective-permute-start.46) | collective-permute-done | bytes 524320 | tf_op jit(solution)/shard_map/ppermute | solution.py:46
  378.4 3.9 shard_map.258
  391.4 22.2 %collective-permute-done.48 = bf16[256,1024]{1,0:T(8,128)(2,1)S(1)} collective-permute-done((bf16[256,1024]{1,0:T(8,128)(2,1)S(1)}, bf16[256,1024]{1,0:T(8,128)(2,1)S(1)}, u32[]{:S(2)}, u32[]{:S(2)}) %collective-permute-start.48) | collective-permute-done | bytes 524320 | tf_op jit(solution)/shard_map/ppermute | solution.py:46
  415.7 5.2 shard_map.259
  427.1 12.6 %shard_map.260 = (f32[1024,256]{1,0:T(8,128)}, f32[1024,256]{1,0:T(8,128)}, bf16[4,256,256]{2,1,0:T(8,128)(2,1)}) custom-call(bf16[1024,256]{1,0:T(8,128)(2,1)} %add_convert_fusion.3.d_att, bf16[2,1024,128]{2,1,0:T(8,128)(2,1)} %get-tuple-element.169.q, bf16[2,1024,128]{2,1,0:T(8,128)(2,1)} %get-tuple-element.170.k, ...), custom_call_target="tpu_custom_call" | custom-call | flops 2684354560 | bytes 8388608 | tf_op jit(solution)/shard_map/pallas_call | solution.py:618
  439.6 4.7 shard_map.261
  458.3 10.6 %shard_map.262 = (bf16[1024,768]{1,0:T(8,128)(2,1)}, bf16[1024,1024]{1,0:T(8,128)(2,1)}, f32[1024,1024]{1,0:T(8,128)}, f32[1,2048]{1,0:T(1,128)}) custom-call(f32[1024,256]{1,0:T(8,128)} %get-tuple-element.174.d_q, f32[1024,256]{1,0:T(8,128)} %get-tuple-element.175.d_k, bf16[4,256,256]{2,1,0:T(8,128)(2,1)} %get-tuple-element.176.d_v, ...), custom_call_target="tpu_custom_call" | custom-call | flops 3221225472 | bytes 20971520 | tf_op jit(solution)/shard_map/pallas_call | solution.py:217
  472.6 4.9 shard_map.265
  484.4 8.8 %shard_map.264 = bf16[2048,768]{1,0:T(8,128)(2,1)} custom-call(bf16[1024,2048]{1,0:T(8,128)(2,1)} %get-tuple-element.120.tokens, f32[1024,1]{1,0:T(8,128)} %get-tuple-element.180.rstd, f32[1,2048]{1,0:T(1,128)} %bitcast.347, bf16[1024,768]{1,0:T(8,128)(2,1)} %get-tuple-element.193.d_qkv), custom_call_target="tpu_custom_call" | custom-call | flops 3221225472 | bytes 16777216 | tf_op jit(solution)/shard_map/pallas_call | solution.py:492
  493.2 3.6 reverse_select_fusion
  507.6 10.4 %collective-permute-done.60.second = bf16[256,1024]{1,0:T(8,128)(2,1)S(1)} collective-permute-done((bf16[256,1024]{1,0:T(8,128)(2,1)}, bf16[256,1024]{1,0:T(8,128)(2,1)S(1)}, u32[]{:S(2)}, u32[]{:S(2)}) %collective-permute-start.60) | collective-permute-done | bytes 524320 | tf_op jit(solution)/shard_map/ppermute | solution.py:46
  520.6 10.4 %collective-permute-done.62.fourth = bf16[256,1024]{1,0:T(8,128)(2,1)S(1)} collective-permute-done((bf16[256,1024]{1,0:T(8,128)(2,1)S(1)}, bf16[256,1024]{1,0:T(8,128)(2,1)S(1)}, u32[]{:S(2)}, u32[]{:S(2)}) %collective-permute-start.62) | collective-permute-done | bytes 524320 | tf_op jit(solution)/shard_map/ppermute | solution.py:46
  541.5 6.6 %collective-permute-done.63 = bf16[128,1024]{1,0:T(8,128)(2,1)S(1)} collective-permute-done((bf16[128,1024]{1,0:T(8,128)(2,1)S(1)}, bf16[128,1024]{1,0:T(8,128)(2,1)S(1)}, u32[]{:S(2)}, u32[]{:S(2)}) %collective-permute-start.63) | collective-permute-done | bytes 262176 | tf_op jit(solution)/shard_map/ppermute | solution.py:109
  548.2 8.3 %collective-permute-done.66 = bf16[128,1024]{1,0:T(8,128)(2,1)S(1)} collective-permute-done((bf16[128,1024]{1,0:T(8,128)(2,1)S(1)}, bf16[128,1024]{1,0:T(8,128)(2,1)S(1)}, u32[]{:S(2)}, u32[]{:S(2)}) %collective-permute-start.66) | collective-permute-done | bytes 262176 | tf_op jit(solution)/shard_map/ppermute | solution.py:109
  558.9 3.4 shard_map.266
  562.3 51.4 %reduce-scatter.8.cloned.1.call-done = bf16[128,1152]{1,0:T(8,128)(2,1)} async-done(((bf16[2048,1152]{1,0:T(8,128)(2,1)}), bf16[128,1152]{1,0:T(8,128)(2,1)}) %reduce-scatter.8.cloned.1.call-update) | async-done | bytes 294928 | tf_op jit(solution)/shard_map/reduce_scatter | solution.py:1103
  (524 shorter events, 229.9 us)
Async XLA Ops:
  7.2 84.9 %all-gather.6.cloned.1.call-start = ((), (), s32[]{:S(2)}) async-start(), calls=%async_computation.3 | async-start | bytes 5013504 | tf_op jit(solution)/shard_map/all_gather | solution.py:937
  36.3 194.2 %all-gather.8.cloned.1.call-start = ((), (), s32[]{:S(2)}) async-start(), calls=%async_computation.7 | async-start | bytes 13369344 | tf_op jit(solution)/shard_map/all_gather | solution.py:940
  41.5 243.5 %all-gather.10.cloned.1.call-start = ((), (), s32[]{:S(2)}) async-start(), calls=%async_computation.8 | async-start | bytes 13369344 | tf_op jit(solution)/shard_map/all_gather | solution.py:940
  42.2 384.8 %reduce-scatter.4.cloned.1.call-start = ((), (), s32[]{:S(2)}) async-start(), calls=%async_computation.4 | async-start | bytes 13369344 | tf_op jit(solution)/shard_map/reduce_scatter | solution.py:1022
  63.5 26.4 %collective-permute-start.4 = (bf16[256,1024]{1,0:T(8,128)(2,1)}, bf16[256,1024]{1,0:T(8,128)(2,1)}, u32[]{:S(2)}, u32[]{:S(2)}) collective-permute-start(bf16[256,1024]{1,0:T(8,128)(2,1)} %pad_maximum_fusion.5.refs_0_), channel_id=1, source_target_pairs={{0,32},{32,64},{64,96},{96,0},{1,33},{33,65},{65,97},{97,1},{2,34}... | collective-permute-start | bytes 1572872 | tf_op jit(solution)/shard_map/ppermute | solution.py:46
  63.7 26.2 %collective-permute-start.5 = (bf16[256,1024]{1,0:T(8,128)(2,1)}, bf16[256,1024]{1,0:T(8,128)(2,1)}, u32[]{:S(2)}, u32[]{:S(2)}) collective-permute-start(bf16[256,1024]{1,0:T(8,128)(2,1)} %pad_maximum_fusion.5.refs_0_), channel_id=1, source_target_pairs={{0,64},{32,96},{64,0},{96,32},{1,65},{33,97},{65,1},{97,33},{2,66}... | collective-permute-start | bytes 1572872 | tf_op jit(solution)/shard_map/ppermute | solution.py:46
  66.5 24.1 %collective-permute-start.6 = (bf16[256,1024]{1,0:T(8,128)(2,1)}, bf16[256,1024]{1,0:T(8,128)(2,1)}, u32[]{:S(2)}, u32[]{:S(2)}) collective-permute-start(bf16[256,1024]{1,0:T(8,128)(2,1)} %pad_maximum_fusion.5.refs_0_), channel_id=1, source_target_pairs={{0,96},{32,0},{64,32},{96,64},{1,97},{33,1},{65,33},{97,65},{2,98}... | collective-permute-start | bytes 1572872 | tf_op jit(solution)/shard_map/ppermute | solution.py:46
  67.6 38.2 %collective-permute-start.7 = (bf16[256,1024]{1,0:T(8,128)(2,1)}, bf16[256,1024]{1,0:T(8,128)(2,1)}, u32[]{:S(2)}, u32[]{:S(2)}) collective-permute-start(bf16[256,1024]{1,0:T(8,128)(2,1)} %pad_maximum_fusion.5.refs_0_), channel_id=1, source_target_pairs={{0,1},{1,0},{2,3},{3,2},{4,5},{5,4},{6,7},{7,6},{8,9},{9,8},{10,11... | collective-permute-start | bytes 1572872 | tf_op jit(solution)/shard_map/ppermute | solution.py:42
  90.5 58.9 %collective-permute-start.25 = (bf16[256,1024]{1,0:T(8,128)(2,1)}, bf16[256,1024]{1,0:T(8,128)(2,1)}, u32[]{:S(2)}, u32[]{:S(2)}) collective-permute-start(bf16[256,1024]{1,0:T(8,128)(2,1)} %pad_maximum_fusion.6), channel_id=1, source_target_pairs={{0,32},{32,64},{64,96},{96,0},{1,33},{33,65},{65,97},{97,1},{2,34}... | collective-permute-start | bytes 1572872 | tf_op jit(solution)/shard_map/ppermute | solution.py:46
  91.4 17.7 %collective-permute-start.10 = (bf16[256,1024]{1,0:T(8,128)(2,1)}, bf16[256,1024]{1,0:T(8,128)(2,1)}, u32[]{:S(2)}, u32[]{:S(2)}) collective-permute-start(bf16[256,1024]{1,0:T(8,128)(2,1)} %collective-permute-done.6.refs_3_), channel_id=1, source_target_pairs={{0,1},{1,0},{2,3},{3,2},{4,5},{5,4},{6,7},{7,6},{8,9},{9,8},{10,11... | collective-permute-start | bytes 1572872 | tf_op jit(solution)/shard_map/ppermute | solution.py:42
  91.4 17.7 %collective-permute-start.8 = (bf16[256,1024]{1,0:T(8,128)(2,1)}, bf16[256,1024]{1,0:T(8,128)(2,1)}, u32[]{:S(2)}, u32[]{:S(2)}) collective-permute-start(bf16[256,1024]{1,0:T(8,128)(2,1)} %collective-permute-done.4.refs_1_), channel_id=1, source_target_pairs={{0,1},{1,0},{2,3},{3,2},{4,5},{5,4},{6,7},{7,6},{8,9},{9,8},{10,11... | collective-permute-start | bytes 1572872 | tf_op jit(solution)/shard_map/ppermute | solution.py:42
  91.9 17.1 %collective-permute-start.9 = (bf16[256,1024]{1,0:T(8,128)(2,1)}, bf16[256,1024]{1,0:T(8,128)(2,1)}, u32[]{:S(2)}, u32[]{:S(2)}) collective-permute-start(bf16[256,1024]{1,0:T(8,128)(2,1)} %collective-permute-done.5.refs_2_), channel_id=1, source_target_pairs={{0,1},{1,0},{2,3},{3,2},{4,5},{5,4},{6,7},{7,6},{8,9},{9,8},{10,11... | collective-permute-start | bytes 1572872 | tf_op jit(solution)/shard_map/ppermute | solution.py:42
  105.8 43.6 %collective-permute-start.26 = (bf16[256,1024]{1,0:T(8,128)(2,1)}, bf16[256,1024]{1,0:T(8,128)(2,1)S(1)}, u32[]{:S(2)}, u32[]{:S(2)}) collective-permute-start(bf16[256,1024]{1,0:T(8,128)(2,1)} %pad_maximum_fusion.6), channel_id=1, source_target_pairs={{0,64},{32,96},{64,0},{96,32},{1,65},{33,97},{65,1},{97,33},{2,66}... | collective-permute-start | bytes 1572872 | tf_op jit(solution)/shard_map/ppermute | solution.py:46
  130.8 18.7 %collective-permute-start.27 = (bf16[256,1024]{1,0:T(8,128)(2,1)}, bf16[256,1024]{1,0:T(8,128)(2,1)S(1)}, u32[]{:S(2)}, u32[]{:S(2)}) collective-permute-start(bf16[256,1024]{1,0:T(8,128)(2,1)} %pad_maximum_fusion.6), channel_id=1, source_target_pairs={{0,96},{32,0},{64,32},{96,64},{1,97},{33,1},{65,33},{97,65},{2,98}... | collective-permute-start | bytes 1572872 | tf_op jit(solution)/shard_map/ppermute | solution.py:46
  161.8 16.5 %collective-permute-start.30 = (bf16[256,1024]{1,0:T(8,128)(2,1)S(1)}, bf16[256,1024]{1,0:T(8,128)(2,1)}, u32[]{:S(2)}, u32[]{:S(2)}) collective-permute-start(bf16[256,1024]{1,0:T(8,128)(2,1)S(1)} %get-tuple-element.245), channel_id=1, source_target_pairs={{0,64},{32,96},{64,0},{96,32},{1,65},{33,97},{65,1},{97,33},{2,66}... | collective-permute-start | bytes 1572872 | tf_op jit(solution)/shard_map/ppermute | solution.py:46
  162.7 25.6 %collective-permute-start.31 = (bf16[256,1024]{1,0:T(8,128)(2,1)S(1)}, bf16[256,1024]{1,0:T(8,128)(2,1)}, u32[]{:S(2)}, u32[]{:S(2)}) collective-permute-start(bf16[256,1024]{1,0:T(8,128)(2,1)S(1)} %get-tuple-element.244), channel_id=1, source_target_pairs={{0,32},{32,64},{64,96},{96,0},{1,33},{33,65},{65,97},{97,1},{2,34}... | collective-permute-start | bytes 1572872 | tf_op jit(solution)/shard_map/ppermute | solution.py:46
  195.4 26.8 %collective-permute-start.34 = (bf16[256,1024]{1,0:T(8,128)(2,1)S(1)}, bf16[256,1024]{1,0:T(8,128)(2,1)S(1)}, u32[]{:S(2)}, u32[]{:S(2)}) collective-permute-start(bf16[256,1024]{1,0:T(8,128)(2,1)S(1)} %multiply_convert_fusion.normed), channel_id=1, source_target_pairs={{0,32},{32,64},{64,96},{96,0},{1,33},{33,65},{65,97},{97,1},{2,34}... | collective-permute-start | bytes 1572872 | tf_op jit(solution)/shard_map/ppermute | solution.py:46
  195.5 26.8 %collective-permute-start.35 = (bf16[256,1024]{1,0:T(8,128)(2,1)S(1)}, bf16[256,1024]{1,0:T(8,128)(2,1)S(1)}, u32[]{:S(2)}, u32[]{:S(2)}) collective-permute-start(bf16[256,1024]{1,0:T(8,128)(2,1)S(1)} %multiply_convert_fusion.normed), channel_id=1, source_target_pairs={{0,64},{32,96},{64,0},{96,32},{1,65},{33,97},{65,1},{97,33},{2,66}... | collective-permute-start | bytes 1572872 | tf_op jit(solution)/shard_map/ppermute | solution.py:46
  197.5 25.4 %collective-permute-start.36 = (bf16[256,1024]{1,0:T(8,128)(2,1)S(1)}, bf16[256,1024]{1,0:T(8,128)(2,1)S(1)}, u32[]{:S(2)}, u32[]{:S(2)}) collective-permute-start(bf16[256,1024]{1,0:T(8,128)(2,1)S(1)} %multiply_convert_fusion.normed), channel_id=1, source_target_pairs={{0,96},{32,0},{64,32},{96,64},{1,97},{33,1},{65,33},{97,65},{2,98}... | collective-permute-start | bytes 1572872 | tf_op jit(solution)/shard_map/ppermute | solution.py:46
  282.6 253.6 %reduce-scatter.6.cloned.1.call-start = ((), (), s32[]{:S(2)}) async-start(), calls=%async_computation.5 | async-start | bytes 13369344 | tf_op jit(solution)/shard_map/reduce_scatter | solution.py:1022
  338.6 275.0 %reduce-scatter.8.cloned.1.call-start = ((), (), s32[]{:S(2)}) async-start(), calls=%async_computation.6 | async-start | bytes 5013504 | tf_op jit(solution)/shard_map/reduce_scatter | solution.py:1103
  350.9 16.3 %collective-permute-start.45 = (bf16[256,1024]{1,0:T(8,128)(2,1)S(1)}, bf16[256,1024]{1,0:T(8,128)(2,1)S(1)}, u32[]{:S(2)}, u32[]{:S(2)}) collective-permute-start(bf16[256,1024]{1,0:T(8,128)(2,1)S(1)} %get-tuple-element.241), channel_id=1, source_target_pairs={{0,64},{32,96},{64,0},{96,32},{1,65},{33,97},{65,1},{97,33},{2,66}... | collective-permute-start | bytes 1572872 | tf_op jit(solution)/shard_map/ppermute | solution.py:46
  352.5 25.1 %collective-permute-start.46 = (bf16[256,1024]{1,0:T(8,128)(2,1)S(1)}, bf16[256,1024]{1,0:T(8,128)(2,1)S(1)}, u32[]{:S(2)}, u32[]{:S(2)}) collective-permute-start(bf16[256,1024]{1,0:T(8,128)(2,1)S(1)} %get-tuple-element.240), channel_id=1, source_target_pairs={{0,32},{32,64},{64,96},{96,0},{1,33},{33,65},{65,97},{97,1},{2,34}... | collective-permute-start | bytes 1572872 | tf_op jit(solution)/shard_map/ppermute | solution.py:46
  387.2 26.5 %collective-permute-start.48 = (bf16[256,1024]{1,0:T(8,128)(2,1)S(1)}, bf16[256,1024]{1,0:T(8,128)(2,1)S(1)}, u32[]{:S(2)}, u32[]{:S(2)}) collective-permute-start(bf16[256,1024]{1,0:T(8,128)(2,1)S(1)} %get-tuple-element.223), channel_id=1, source_target_pairs={{0,32},{32,64},{64,96},{96,0},{1,33},{33,65},{65,97},{97,1},{2,34}... | collective-permute-start | bytes 1572872 | tf_op jit(solution)/shard_map/ppermute | solution.py:46
  387.3 26.3 %collective-permute-start.49 = (bf16[256,1024]{1,0:T(8,128)(2,1)S(1)}, bf16[256,1024]{1,0:T(8,128)(2,1)S(1)}, u32[]{:S(2)}, u32[]{:S(2)}) collective-permute-start(bf16[256,1024]{1,0:T(8,128)(2,1)S(1)} %get-tuple-element.223), channel_id=1, source_target_pairs={{0,64},{32,96},{64,0},{96,32},{1,65},{33,97},{65,1},{97,33},{2,66}... | collective-permute-start | bytes 1572872 | tf_op jit(solution)/shard_map/ppermute | solution.py:46
  389.5 24.7 %collective-permute-start.50 = (bf16[256,1024]{1,0:T(8,128)(2,1)S(1)}, bf16[256,1024]{1,0:T(8,128)(2,1)S(1)}, u32[]{:S(2)}, u32[]{:S(2)}) collective-permute-start(bf16[256,1024]{1,0:T(8,128)(2,1)S(1)} %get-tuple-element.223), channel_id=1, source_target_pairs={{0,96},{32,0},{64,32},{96,64},{1,97},{33,1},{65,33},{97,65},{2,98}... | collective-permute-start | bytes 1572872 | tf_op jit(solution)/shard_map/ppermute | solution.py:46
  422.1 29.1 %collective-permute-start.56 = (bf16[256,1024]{1,0:T(8,128)(2,1)}, bf16[256,1024]{1,0:T(8,128)(2,1)}, u32[]{:S(2)}, u32[]{:S(2)}) collective-permute-start(bf16[256,1024]{1,0:T(8,128)(2,1)} %get-tuple-element.237), channel_id=1, source_target_pairs={{0,96},{32,0},{64,32},{96,64},{1,97},{33,1},{65,33},{97,65},{2,98}... | collective-permute-start | bytes 1572872 | tf_op jit(solution)/shard_map/ppermute | solution.py:46
  425.2 26.0 %collective-permute-start.57 = (bf16[256,1024]{1,0:T(8,128)(2,1)}, bf16[256,1024]{1,0:T(8,128)(2,1)}, u32[]{:S(2)}, u32[]{:S(2)}) collective-permute-start(bf16[256,1024]{1,0:T(8,128)(2,1)} %get-tuple-element.239), channel_id=1, source_target_pairs={{0,64},{32,96},{64,0},{96,32},{1,65},{33,97},{65,1},{97,33},{2,66}... | collective-permute-start | bytes 1572872 | tf_op jit(solution)/shard_map/ppermute | solution.py:46
  425.6 26.3 %collective-permute-start.58 = (bf16[256,1024]{1,0:T(8,128)(2,1)}, bf16[256,1024]{1,0:T(8,128)(2,1)}, u32[]{:S(2)}, u32[]{:S(2)}) collective-permute-start(bf16[256,1024]{1,0:T(8,128)(2,1)} %get-tuple-element.238), channel_id=1, source_target_pairs={{0,32},{32,64},{64,96},{96,0},{1,33},{33,65},{65,97},{97,1},{2,34}... | collective-permute-start | bytes 1572872 | tf_op jit(solution)/shard_map/ppermute | solution.py:46
  504.0 16.5 %collective-permute-start.61 = (bf16[256,1024]{1,0:T(8,128)(2,1)}, bf16[256,1024]{1,0:T(8,128)(2,1)S(1)}, u32[]{:S(2)}, u32[]{:S(2)}) collective-permute-start(bf16[256,1024]{1,0:T(8,128)(2,1)} %get-tuple-element.234), channel_id=1, source_target_pairs={{0,64},{32,96},{64,0},{96,32},{1,65},{33,97},{65,1},{97,33},{2,66}... | collective-permute-start | bytes 1572872 | tf_op jit(solution)/shard_map/ppermute | solution.py:46
  504.5 26.4 %collective-permute-start.62 = (bf16[256,1024]{1,0:T(8,128)(2,1)S(1)}, bf16[256,1024]{1,0:T(8,128)(2,1)S(1)}, u32[]{:S(2)}, u32[]{:S(2)}) collective-permute-start(bf16[256,1024]{1,0:T(8,128)(2,1)S(1)} %get-tuple-element.233), channel_id=1, source_target_pairs={{0,32},{32,64},{64,96},{96,0},{1,33},{33,65},{65,97},{97,1},{2,34}... | collective-permute-start | bytes 1572872 | tf_op jit(solution)/shard_map/ppermute | solution.py:46
  539.4 17.1 %collective-permute-start.66 = (bf16[128,1024]{1,0:T(8,128)(2,1)S(1)}, bf16[128,1024]{1,0:T(8,128)(2,1)S(1)}, u32[]{:S(2)}, u32[]{:S(2)}) collective-permute-start(bf16[128,1024]{1,0:T(8,128)(2,1)S(1)} %broadcast_select_fusion.1), channel_id=1, source_target_pairs={{0,16},{16,0},{1,17},{17,1},{2,18},{18,2},{3,19},{19,3},{4,20},{20... | collective-permute-start | bytes 786440 | tf_op jit(solution)/shard_map/ppermute | solution.py:109
  (89 other events, 814.9 us)
Sparse Core Ops, SparseCore 0:
  36.4 54.9 all-gather.5
  93.6 89.7 all-gather.7
  185.5 89.7 all-gather.9
  282.7 93.2 reduce-scatter.3
  379.3 93.7 reduce-scatter.5
  536.3 77.2 reduce-scatter.7

commit v2 on v1

--- a/solution.py
+++ b/solution.py
@@ -93,16 +93,44 @@
     return [jnp.asarray(table, jnp.float32) for table in tables]
 
 
+def plane_and_ring_sum(a, ring, z, x):
+    depth = ("zh", "zl")
+
+    def pieces(b, dim, me):
+        return [
+            lax.dynamic_index_in_dim(b, (me + step) % 4, dim, keepdims=False) for step in range(4)
+        ]
+
+    def moved(parts, axes):
+        return [parts[0]] + [
+            lax.ppermute(parts[step], axes, [(i, (i + step) % 4) for i in range(4)])
+            for step in (1, 2, 3)
+        ]
+
+    def summed(parts):
+        first, second, third, fourth = [f32(part) for part in parts]
+        return bf16(((first + second) + third) + fourth)
+
+    low, high = pieces(a[:, :, :64], 1, x), pieces(a[:, :, 64:], 0, z)
+    low, high, ring = lax.optimization_barrier((low, high, ring))
+    ring = y_scatter(ring)
+    low, high = moved(low, "x"), moved(high, depth)
+    low, high, ring = lax.optimization_barrier((low, high, ring))
+    low, high = pieces(summed(low), 0, z), pieces(summed(high), 0, x)
+    low, high = lax.optimization_barrier((low, high))
+    return jnp.concatenate([summed(moved(low, depth)), summed(moved(high, "x"))]), ring
+
+
 def split_halves(a):
-    blocks = [a[..., k * 128 : k * 128 + 128] for k in range(a.shape[-1] // 128)]
-    return jnp.concatenate(blocks[0::2], axis=-1), jnp.concatenate(blocks[1::2], axis=-1)
+    lead = a.shape[:-1]
+    pairs = a.reshape(*lead, a.shape[-1] // 256, 2, 128)
+    return pairs[..., 0, :].reshape(*lead, -1), pairs[..., 1, :].reshape(*lead, -1)
 
 
 def join_halves(low, high):
-    blocks = []
-    for k in range(low.shape[-1] // 128):
-        blocks += [low[..., k * 128 : k * 128 + 128], high[..., k * 128 : k * 128 + 128]]
-    return jnp.concatenate(blocks, axis=-1)
+    lead = low.shape[:-1]
+    pairs = jnp.stack([low.reshape(*lead, -1, 128), high.reshape(*lead, -1, 128)], axis=-2)
+    return pairs.reshape(*lead, -1)
 
 
 def other_layer(a):
@@ -1066,18 +1094,11 @@
     )
     grad_norm_attn = grad_norm_attn.reshape(D)
     received = other_core(d_par)
-    received, d_qkv = lax.optimization_barrier((received, d_qkv))
+    received, d_qkv, expert_grads[1] = lax.optimization_barrier(
+        (received, d_qkv, expert_grads[1])
+    )
     d_sent = bf16(d_own + f32(received))
-    got = y_scatter([d_sent[s * 256 : s * 256 + 256] for s in range(4)])
     grad_qkv = outer(x_all, rstd_one, gain_attn.reshape(1, D), d_qkv)
-    got, moe_here = lax.optimization_barrier((got, moe_here))
-    layer_output = from_half(bf16(after + moe_here), zh, c)[None]
-    hat_here = x_here * rstd_one[:256]
-    d_normed_one, along = back_sums(x_all, rstd_one, gain_attn[:1], got)
-    along = along.reshape(256)
-    along = (along + other_core(along))[:, None] / D
-    grad_tokens = bf16(d_after + rstd_one[:256] * (d_normed_one - hat_here * along))
-
     wide = jnp.concatenate([grad_norm_moe[:, None], grad_router], axis=1)
     wide = jnp.pad(wide, ((0, HALF), (0, 0)))
     extras = jnp.concatenate([grad_norm_attn[:, None], wide], axis=1).reshape(2, HALF, 18)
@@ -1099,8 +1120,20 @@
     grad_out = jnp.where(own_first, grad_out, grad_out[::-1]).reshape(16, 32, 4, 256)
     grad_out = grad_out.transpose(0, 2, 1, 3).reshape(16, 128, 256)
     both = jnp.concatenate([both, grad_out], axis=2).reshape(D, 1152)
-    both, expert_grads, got = lax.optimization_barrier((both, expert_grads, got))
-    both = lax.psum_scatter(both, plane, scatter_dimension=0, tiled=True)
+    both, got = plane_and_ring_sum(
+        both.reshape(4, 4, 128, 1152),
+        [d_sent[s * 256 : s * 256 + 256] for s in range(4)],
+        zh * 2 + lax.axis_index("zl"),
+        lax.axis_index("x"),
+    )
+    got, moe_here = lax.optimization_barrier((got, moe_here))
+    layer_output = from_half(bf16(after + moe_here), zh, c)[None]
+    hat_here = x_here * rstd_one[:256]
+    d_normed_one, along = back_sums(x_all, rstd_one, gain_attn[:1], got)
+    along = along.reshape(256)
+    along = (along + other_core(along))[:, None] / D
+    grad_tokens = bf16(d_after + rstd_one[:256] * (d_normed_one - hat_here * along))
+
     grad_out = both[:, 896:].reshape(4, 32, 256).transpose(1, 0, 2).reshape(32, HALF)
     both = f32(trade(both[:, :896].reshape(8, 16, 896), y, c))
     grad_w_qkv = both[:, :, :768].reshape(8, 16, 3, 256).transpose(1, 2, 0, 3).reshape(16, 3 * D)

time: 647 us -> 635 us (0.981)
  waiting for transfers between devices: 250 us -> 206 us
  starting transfers between devices: 74.9 us -> 98 us
  other arithmetic: 47.2 us -> 54 us
    reduce_scatter x1 -> x0, waiting for transfers between devices: 51.4 us -> none  [on_device(): both = lax.psum_scatter(both, plane, scatter_dimension=0, tiled=True)]
    ppermute x0 -> x12, waiting for transfers between devices: none -> 24 us  [moved(): lax.ppermute(parts[step], axes, [(i, (i + step) % 4) for i in range(4)])]
    ppermute x0 -> x12, starting transfers between devices: none -> 17.9 us  [moved(): lax.ppermute(parts[step], axes, [(i, (i + step) % 4) for i in range(4)])]
    ppermute x5, waiting for transfers between devices: 22.7 us -> 9.03 us  [other_layer(): return lax.ppermute(a, 'zh', [(0, 1), (1, 0)])]
    convert_element_type x8 -> x12, other arithmetic: 9.56 us -> 17.5 us  [bf16(): return a.astype(jnp.bfloat16)]
    unnamed x172 -> x126, local copies, waits for them, and re-layouts: 20.7 us -> 15.5 us
  transfers between devices with their start and end apart: 79 -> 90, of which waited for: 45 -> 45; matrix products, arithmetic and copies ran while one was open for 15% -> 15% of each run, Pallas kernels for 29% -> 28%
where the time goes in v2:
time: 635 us; the launch traced here: 629 us
  waiting for transfers between devices  206 us (32%)
  Pallas kernels  183 us (29%)
  starting transfers between devices  98 us (15%)
  local copies, waits for them, and re-layouts  71 us (11%)
  other arithmetic  54 us (9%)
  between operations  16.4 us (3%)
    ppermute x42, waiting for transfers between devices, from_chip(): return lax.ppermute(a, 'y', [(i, (i + step) % 4) for i in range(4)])  147 us
    ppermute x42, starting transfers between devices, from_chip(): return lax.ppermute(a, 'y', [(i, (i + step) % 4) for i in range(4)])  61.3 us
    pallas_call x2, Pallas kernels, close_experts(): pl.pallas_call(body, grid=(2, CHUNKS), in_specs=[line, part, part, slot_t...  55 us
    pallas_call x2, Pallas kernels, open_experts(): pl.pallas_call(open_kernel, grid=(2, CHUNKS), in_specs=[line, line, whole...  33.3 us
    ppermute x26, waiting for transfers between devices, other_core(): return lax.ppermute(a, 'c', [(0, 1), (1, 0)])  25.4 us
    ppermute x12, waiting for transfers between devices, moved(): lax.ppermute(parts[step], axes, [(i, (i + step) % 4) for i in range(4)])  24 us
    ppermute x12, starting transfers between devices, moved(): lax.ppermute(parts[step], axes, [(i, (i + step) % 4) for i in range(4)])  17.9 us
    convert_element_type x12, other arithmetic, bf16(): return a.astype(jnp.bfloat16)  17.5 us
  transfers between devices with their start and end apart: 90, of which 45 were waited for; matrix products, arithmetic and copies ran while one was open for 15% of the time, Pallas kernels for 28%

profile of v2, /device:TPU:32, one launch (start us, length us, event | category | flops | bytes accessed | tf_op | source)
XLA Modules:
  0.0 628.6 jit_solution(11401262566755667539)
XLA Ops:
  27.9 4.5 collective-permute-done.1
  46.5 3.6 collective-permute-start.19
  68.6 18.6 %collective-permute-done.4.refs_1_ = bf16[256,1024]{1,0:T(8,128)(2,1)} collective-permute-done((bf16[256,1024]{1,0:T(8,128)(2,1)}, bf16[256,1024]{1,0:T(8,128)(2,1)}, u32[]{:S(2)}, u32[]{:S(2)}) %collective-permute-start.4) | collective-permute-done | bytes 524320 | tf_op jit(solution)/shard_map/ppermute | solution.py:46
  106.1 10.1 %shard_map.248 = (f32[1024,768]{1,0:T(8,128)}, bf16[1024,2048]{1,0:T(8,128)(2,1)}, f32[1024,1]{1,0:T(8,128)}, f32[16,1024]{1,0:T(8,128)}) custom-call(bf16[256,1024]{1,0:T(8,128)(2,1)} %pad_maximum_fusion.4.refs_0_, bf16[256,1024]{1,0:T(8,128)(2,1)} %collective-permute-done.4.refs_1_, bf16[256,1024]{1,0:T(8,128)(2,1)} %collective-permute-done.5.refs_2_, ...), custom_call_target="tpu_custom_call" | custom-call | flops 3221225472 | bytes 20971520 | tf_op jit(solution)/shard_map/pallas_call | solution.py:192
  133.5 13.2 %shard_map.249 = (bf16[4,256,256]{2,1,0:T(8,128)(2,1)}, bf16[2,1024,128]{2,1,0:T(8,128)(2,1)}, bf16[2,1024,128]{2,1,0:T(8,128)(2,1)}, bf16[2,1024,128]{2,1,0:T(8,128)(2,1)}, f32[2,1,1024]{2,1,0:T(1,128)}) custom-call(f32[1024,768]{1,0:T(8,128)} %get-tuple-element.153.q_pre.k_pre.v_pre, f32[1024,768]{1,0:T(8,128)} %get-tuple-element.153.q_pre.k_pre.v_pre, ...), custom_call_target="tpu_custom_call" | custom-call | flops 1073741824 | bytes 8388608 | tf_op jit(solution)/shard_map/pallas_call | solution.py:567
  150.9 5.2 shard_map.250
  161.4 11.2 %collective-permute-done.29.first = bf16[256,1024]{1,0:T(8,128)(2,1)} collective-permute-done((bf16[256,1024]{1,0:T(8,128)(2,1)S(1)}, bf16[256,1024]{1,0:T(8,128)(2,1)}, u32[]{:S(2)}, u32[]{:S(2)}) %collective-permute-start.29) | collective-permute-done | bytes 524320 | tf_op jit(solution)/shard_map/ppermute | solution.py:46
  175.6 10.1 %collective-permute-done.31.third = bf16[256,1024]{1,0:T(8,128)(2,1)} collective-permute-done((bf16[256,1024]{1,0:T(8,128)(2,1)S(1)}, bf16[256,1024]{1,0:T(8,128)(2,1)}, u32[]{:S(2)}, u32[]{:S(2)}) %collective-permute-start.31) | collective-permute-done | bytes 524320 | tf_op jit(solution)/shard_map/ppermute | solution.py:46
  199.9 19.7 %collective-permute-done.34 = bf16[256,1024]{1,0:T(8,128)(2,1)S(1)} collective-permute-done((bf16[256,1024]{1,0:T(8,128)(2,1)S(1)}, bf16[256,1024]{1,0:T(8,128)(2,1)S(1)}, u32[]{:S(2)}, u32[]{:S(2)}) %collective-permute-start.34) | collective-permute-done | bytes 524320 | tf_op jit(solution)/shard_map/ppermute | solution.py:46
  228.2 16.8 %shard_map.254 = (bf16[2,384,3072]{2,1,0:T(8,128)(2,1)}, bf16[2,1024,384]{2,1,0:T(8,128)(2,1)}, bf16[2,1024,384]{2,1,0:T(8,128)(2,1)}, bf16[2,384,1024]{2,1,0:T(...) custom-call(s32[2,1,1024]{2,1,0:T(1,128)} %compare_select_fusion.4.seat.refs_0_, ...), custom_call_target="tpu_custom_call" | custom-call | flops 8053063680 | bytes 31457280 | tf_op jit(solution)/shard_map/pallas_call | solution.py:776
  245.5 7.7 %collective-permute-done.38.refs_2_ = bf16[2,384,3072]{2,1,0:T(8,128)(2,1)S(1)} collective-permute-done((bf16[2,384,3072]{2,1,0:T(8,128)(2,1)}, bf16[2,384,3072]{2,1,0:T(8,128)(2,1)S(1)}, u32[]{:S(2)}, u32[]{:S(2)}) %collective-permute-start.38) | collective-permute-done | bytes 4718624 | tf_op jit(solution)/shard_map/ppermute | solution.py:42
  255.5 26.6 %shard_map.255 = (bf16[4,256,1024]{2,1,0:T(8,128)(2,1)}, bf16[4,256,1024]{2,1,0:T(8,128)(2,1)}, bf16[2,1024,3072]{2,1,0:T(8,128)(2,1)}, f32[2,1,1024]{2,1,0:T(1,128)}) custom-call(s32[2,1,1024]{2,1,0:T(1,128)} %compare_select_fusion.4.seat.refs_0_, bf16[2,384,3072]{2,1,0:T(8,128)(2,1)} %get-tuple-element.172.refs_1_, bf16[2,384,3072]{2,1,0:T(8,128)(2,1)} %copy-done.48, ...), custom_call_target="tpu_custom_call" | custom-call | flops 12884901888 | bytes 52428800 | tf_op jit(solution)/shard_map/pallas_call | solution.py:882
  284.5 16.5 %shard_map.256 = (bf16[2,384,3072]{2,1,0:T(8,128)(2,1)}, bf16[2,1024,384]{2,1,0:T(8,128)(2,1)}, bf16[2,1024,384]{2,1,0:T(8,128)(2,1)}, bf16[2,384,1024]{2,1,0:T(...) custom-call(s32[2,1,1024]{2,1,0:T(1,128)} %compare_select_fusion.5.seat.refs_0_, ...), custom_call_target="tpu_custom_call" | custom-call | flops 8053063680 | bytes 31457280 | tf_op jit(solution)/shard_map/pallas_call | solution.py:776
  301.5 7.8 %collective-permute-done.39.refs_2_ = bf16[2,384,3072]{2,1,0:T(8,128)(2,1)S(1)} collective-permute-done((bf16[2,384,3072]{2,1,0:T(8,128)(2,1)}, bf16[2,384,3072]{2,1,0:T(8,128)(2,1)S(1)}, u32[]{:S(2)}, u32[]{:S(2)}) %collective-permute-start.39) | collective-permute-done | bytes 4718624 | tf_op jit(solution)/shard_map/ppermute | solution.py:42
  311.6 28.5 %shard_map.257 = (bf16[4,256,1024]{2,1,0:T(8,128)(2,1)}, bf16[4,256,1024]{2,1,0:T(8,128)(2,1)}, bf16[2,1024,3072]{2,1,0:T(8,128)(2,1)}, f32[2,1,1024]{2,1,0:T(1,128)}) custom-call(s32[2,1,1024]{2,1,0:T(1,128)} %compare_select_fusion.5.seat.refs_0_, bf16[2,384,3072]{2,1,0:T(8,128)(2,1)} %get-tuple-element.181.refs_1_, bf16[2,384,3072]{2,1,0:T(8,128)(2,1)} %copy-done.47, ...), custom_call_target="tpu_custom_call" | custom-call | flops 12884901888 | bytes 52428800 | tf_op jit(solution)/shard_map/pallas_call | solution.py:882
  353.7 10.9 %collective-permute-done.44.refs_1_ = bf16[256,1024]{1,0:T(8,128)(2,1)S(1)} collective-permute-done((bf16[256,1024]{1,0:T(8,128)(2,1)S(1)}, bf16[256,1024]{1,0:T(8,128)(2,1)S(1)}, u32[]{:S(2)}, u32[]{:S(2)}) %collective-permute-start.44) | collective-permute-done | bytes 524320 | tf_op jit(solution)/shard_map/ppermute | solution.py:46
  366.9 10.5 %collective-permute-done.46.refs_3_ = bf16[256,1024]{1,0:T(8,128)(2,1)S(1)} collective-permute-done((bf16[256,1024]{1,0:T(8,128)(2,1)S(1)}, bf16[256,1024]{1,0:T(8,128)(2,1)S(1)}, u32[]{:S(2)}, u32[]{:S(2)}) %collective-permute-start.46) | collective-permute-done | bytes 524320 | tf_op jit(solution)/shard_map/ppermute | solution.py:46
  378.2 3.9 shard_map.258
  391.3 22.1 %collective-permute-done.48 = bf16[256,1024]{1,0:T(8,128)(2,1)S(1)} collective-permute-done((bf16[256,1024]{1,0:T(8,128)(2,1)S(1)}, bf16[256,1024]{1,0:T(8,128)(2,1)S(1)}, u32[]{:S(2)}, u32[]{:S(2)}) %collective-permute-start.48) | collective-permute-done | bytes 524320 | tf_op jit(solution)/shard_map/ppermute | solution.py:46
  415.5 5.3 shard_map.259
  426.6 12.6 %shard_map.260 = (f32[1024,256]{1,0:T(8,128)}, f32[1024,256]{1,0:T(8,128)}, bf16[4,256,256]{2,1,0:T(8,128)(2,1)}) custom-call(bf16[1024,256]{1,0:T(8,128)(2,1)} %add_convert_fusion.5.d_att, bf16[2,1024,128]{2,1,0:T(8,128)(2,1)} %get-tuple-element.200.q, bf16[2,1024,128]{2,1,0:T(8,128)(2,1)} %get-tuple-element.201.k, ...), custom_call_target="tpu_custom_call" | custom-call | flops 2684354560 | bytes 8388608 | tf_op jit(solution)/shard_map/pallas_call | solution.py:646
  439.2 4.7 shard_map.261
  458.0 10.6 %shard_map.262 = (bf16[1024,768]{1,0:T(8,128)(2,1)}, bf16[1024,1024]{1,0:T(8,128)(2,1)}, f32[1024,1024]{1,0:T(8,128)}, f32[1,2048]{1,0:T(1,128)}) custom-call(f32[1024,256]{1,0:T(8,128)} %get-tuple-element.205.d_q, f32[1024,256]{1,0:T(8,128)} %get-tuple-element.206.d_k, bf16[4,256,256]{2,1,0:T(8,128)(2,1)} %get-tuple-element.207.d_v, ...), custom_call_target="tpu_custom_call" | custom-call | flops 3221225472 | bytes 20971520 | tf_op jit(solution)/shard_map/pallas_call | solution.py:245
  469.4 5.0 shard_map.264
  487.0 3.6 add_convert_fusion
  492.0 8.8 %shard_map.263 = bf16[2048,768]{1,0:T(8,128)(2,1)} custom-call(bf16[1024,2048]{1,0:T(8,128)(2,1)} %get-tuple-element.150.tokens, f32[1024,1]{1,0:T(8,128)} %get-tuple-element.164.rstd, f32[1,2048]{1,0:T(1,128)} %bitcast.420, bf16[1024,768]{1,0:T(8,128)(2,1)} %get-tuple-element.214.d_qkv), custom_call_target="tpu_custom_call" | custom-call | flops 3221225472 | bytes 16777216 | tf_op jit(solution)/shard_map/pallas_call | solution.py:520
  500.8 3.6 reverse_select_fusion
  513.1 10.1 %collective-permute-done.66.second = bf16[256,1024]{1,0:T(8,128)(2,1)S(1)} collective-permute-done((bf16[256,1024]{1,0:T(8,128)(2,1)S(1)}, bf16[256,1024]{1,0:T(8,128)(2,1)S(1)}, u32[]{:S(2)}, u32[]{:S(2)}) %collective-permute-start.66) | collective-permute-done | bytes 524320 | tf_op jit(solution)/shard_map/ppermute | solution.py:46
  525.9 10.8 %collective-permute-done.68.fourth = bf16[256,1024]{1,0:T(8,128)(2,1)S(1)} collective-permute-done((bf16[256,1024]{1,0:T(8,128)(2,1)S(1)}, bf16[256,1024]{1,0:T(8,128)(2,1)S(1)}, u32[]{:S(2)}, u32[]{:S(2)}) %collective-permute-start.68) | collective-permute-done | bytes 524320 | tf_op jit(solution)/shard_map/ppermute | solution.py:46
  543.4 11.2 %collective-permute-done.64 = bf16[4,64,1152]{2,1,0:T(8,128)(2,1)} collective-permute-done((bf16[4,64,1152]{2,1,0:T(8,128)(2,1)S(1)}, bf16[4,64,1152]{2,1,0:T(8,128)(2,1)}, u32[]{:S(2)}, u32[]{:S(2)}) %collective-permute-start.64) | collective-permute-done | bytes 589856 | tf_op jit(solution)/shard_map/ppermute | solution.py:106
  554.5 11.5 %collective-permute-done.65 = bf16[4,64,1152]{2,1,0:T(8,128)(2,1)} collective-permute-done((bf16[4,64,1152]{2,1,0:T(8,128)(2,1)S(1)}, bf16[4,64,1152]{2,1,0:T(8,128)(2,1)}, u32[]{:S(2)}, u32[]{:S(2)}) %collective-permute-start.65) | collective-permute-done | bytes 589856 | tf_op jit(solution)/shard_map/ppermute | solution.py:106
  599.6 10.4 %collective-permute-start.82 = (bf16[2,16,896]{2,1,0:T(8,128)(2,1)S(1)}, bf16[2,16,896]{2,1,0:T(8,128)(2,1)S(1)}, u32[]{:S(2)}, u32[]{:S(2)}) collective-permute-start(bf16[2,16,896]{2,1,0:T(8,128)(2,1)S(1)} %get-tuple-element.337), channel_id=1, source_target_pairs={{0,64},{32,96},{64,0},{96,32},{1,65},{33,97},{65,1},{97,33},{2,66}... | collective-permute-start | bytes 172040 | tf_op jit(solution)/shard_map/ppermute | solution.py:46
  (515 shorter events, 256.4 us)
Async XLA Ops:
  7.2 82.0 %all-gather.6.cloned.1.call-start = ((), (), s32[]{:S(2)}) async-start(), calls=%async_computation.2 | async-start | bytes 5013504 | tf_op jit(solution)/shard_map/all_gather | solution.py:965
  33.3 194.9 %all-gather.8.cloned.1.call-start = ((), (), s32[]{:S(2)}) async-start(), calls=%async_computation.5 | async-start | bytes 13369344 | tf_op jit(solution)/shard_map/all_gather | solution.py:968
  38.5 245.9 %all-gather.10.cloned.1.call-start = ((), (), s32[]{:S(2)}) async-start(), calls=%async_computation.6 | async-start | bytes 13369344 | tf_op jit(solution)/shard_map/all_gather | solution.py:968
  39.3 387.3 %reduce-scatter.3.cloned.1.call-start = ((), (), s32[]{:S(2)}) async-start(), calls=%async_computation.3 | async-start | bytes 13369344 | tf_op jit(solution)/shard_map/reduce_scatter | solution.py:1050
  60.1 27.0 %collective-permute-start.4 = (bf16[256,1024]{1,0:T(8,128)(2,1)}, bf16[256,1024]{1,0:T(8,128)(2,1)}, u32[]{:S(2)}, u32[]{:S(2)}) collective-permute-start(bf16[256,1024]{1,0:T(8,128)(2,1)} %pad_maximum_fusion.4.refs_0_), channel_id=1, source_target_pairs={{0,32},{32,64},{64,96},{96,0},{1,33},{33,65},{65,97},{97,1},{2,34}... | collective-permute-start | bytes 1572872 | tf_op jit(solution)/shard_map/ppermute | solution.py:46
  61.0 26.2 %collective-permute-start.5 = (bf16[256,1024]{1,0:T(8,128)(2,1)}, bf16[256,1024]{1,0:T(8,128)(2,1)}, u32[]{:S(2)}, u32[]{:S(2)}) collective-permute-start(bf16[256,1024]{1,0:T(8,128)(2,1)} %pad_maximum_fusion.4.refs_0_), channel_id=1, source_target_pairs={{0,64},{32,96},{64,0},{96,32},{1,65},{33,97},{65,1},{97,33},{2,66}... | collective-permute-start | bytes 1572872 | tf_op jit(solution)/shard_map/ppermute | solution.py:46
  63.7 24.1 %collective-permute-start.6 = (bf16[256,1024]{1,0:T(8,128)(2,1)}, bf16[256,1024]{1,0:T(8,128)(2,1)}, u32[]{:S(2)}, u32[]{:S(2)}) collective-permute-start(bf16[256,1024]{1,0:T(8,128)(2,1)} %pad_maximum_fusion.4.refs_0_), channel_id=1, source_target_pairs={{0,96},{32,0},{64,32},{96,64},{1,97},{33,1},{65,33},{97,65},{2,98}... | collective-permute-start | bytes 1572872 | tf_op jit(solution)/shard_map/ppermute | solution.py:46
  66.9 35.9 %collective-permute-start.7 = (bf16[256,1024]{1,0:T(8,128)(2,1)}, bf16[256,1024]{1,0:T(8,128)(2,1)}, u32[]{:S(2)}, u32[]{:S(2)}) collective-permute-start(bf16[256,1024]{1,0:T(8,128)(2,1)} %pad_maximum_fusion.4.refs_0_), channel_id=1, source_target_pairs={{0,1},{1,0},{2,3},{3,2},{4,5},{5,4},{6,7},{7,6},{8,9},{9,8},{10,11... | collective-permute-start | bytes 1572872 | tf_op jit(solution)/shard_map/ppermute | solution.py:42
  87.8 58.9 %collective-permute-start.25 = (bf16[256,1024]{1,0:T(8,128)(2,1)}, bf16[256,1024]{1,0:T(8,128)(2,1)}, u32[]{:S(2)}, u32[]{:S(2)}) collective-permute-start(bf16[256,1024]{1,0:T(8,128)(2,1)} %pad_maximum_fusion.5), channel_id=1, source_target_pairs={{0,32},{32,64},{64,96},{96,0},{1,33},{33,65},{65,97},{97,1},{2,34}... | collective-permute-start | bytes 1572872 | tf_op jit(solution)/shard_map/ppermute | solution.py:46
  102.9 43.8 %collective-permute-start.26 = (bf16[256,1024]{1,0:T(8,128)(2,1)}, bf16[256,1024]{1,0:T(8,128)(2,1)S(1)}, u32[]{:S(2)}, u32[]{:S(2)}) collective-permute-start(bf16[256,1024]{1,0:T(8,128)(2,1)} %pad_maximum_fusion.5), channel_id=1, source_target_pairs={{0,64},{32,96},{64,0},{96,32},{1,65},{33,97},{65,1},{97,33},{2,66}... | collective-permute-start | bytes 1572872 | tf_op jit(solution)/shard_map/ppermute | solution.py:46
  128.0 18.7 %collective-permute-start.27 = (bf16[256,1024]{1,0:T(8,128)(2,1)}, bf16[256,1024]{1,0:T(8,128)(2,1)S(1)}, u32[]{:S(2)}, u32[]{:S(2)}) collective-permute-start(bf16[256,1024]{1,0:T(8,128)(2,1)} %pad_maximum_fusion.5), channel_id=1, source_target_pairs={{0,96},{32,0},{64,32},{96,64},{1,97},{33,1},{65,33},{97,65},{2,98}... | collective-permute-start | bytes 1572872 | tf_op jit(solution)/shard_map/ppermute | solution.py:46
  160.0 25.6 %collective-permute-start.31 = (bf16[256,1024]{1,0:T(8,128)(2,1)S(1)}, bf16[256,1024]{1,0:T(8,128)(2,1)}, u32[]{:S(2)}, u32[]{:S(2)}) collective-permute-start(bf16[256,1024]{1,0:T(8,128)(2,1)S(1)} %get-tuple-element.312), channel_id=1, source_target_pairs={{0,32},{32,64},{64,96},{96,0},{1,33},{33,65},{65,97},{97,1},{2,34}... | collective-permute-start | bytes 1572872 | tf_op jit(solution)/shard_map/ppermute | solution.py:46
  192.7 26.9 %collective-permute-start.34 = (bf16[256,1024]{1,0:T(8,128)(2,1)S(1)}, bf16[256,1024]{1,0:T(8,128)(2,1)S(1)}, u32[]{:S(2)}, u32[]{:S(2)}) collective-permute-start(bf16[256,1024]{1,0:T(8,128)(2,1)S(1)} %multiply_convert_fusion.normed), channel_id=1, source_target_pairs={{0,32},{32,64},{64,96},{96,0},{1,33},{33,65},{65,97},{97,1},{2,34}... | collective-permute-start | bytes 1572872 | tf_op jit(solution)/shard_map/ppermute | solution.py:46
  192.8 26.8 %collective-permute-start.35 = (bf16[256,1024]{1,0:T(8,128)(2,1)S(1)}, bf16[256,1024]{1,0:T(8,128)(2,1)S(1)}, u32[]{:S(2)}, u32[]{:S(2)}) collective-permute-start(bf16[256,1024]{1,0:T(8,128)(2,1)S(1)} %multiply_convert_fusion.normed), channel_id=1, source_target_pairs={{0,64},{32,96},{64,0},{96,32},{1,65},{33,97},{65,1},{97,33},{2,66}... | collective-permute-start | bytes 1572872 | tf_op jit(solution)/shard_map/ppermute | solution.py:46
  194.8 25.4 %collective-permute-start.36 = (bf16[256,1024]{1,0:T(8,128)(2,1)S(1)}, bf16[256,1024]{1,0:T(8,128)(2,1)S(1)}, u32[]{:S(2)}, u32[]{:S(2)}) collective-permute-start(bf16[256,1024]{1,0:T(8,128)(2,1)S(1)} %multiply_convert_fusion.normed), channel_id=1, source_target_pairs={{0,96},{32,0},{64,32},{96,64},{1,97},{33,1},{65,33},{97,65},{2,98}... | collective-permute-start | bytes 1572872 | tf_op jit(solution)/shard_map/ppermute | solution.py:46
  282.1 204.9 %reduce-scatter.5.cloned.1.call-start = ((), (), s32[]{:S(2)}) async-start(), calls=%async_computation.4 | async-start | bytes 13369344 | tf_op jit(solution)/shard_map/reduce_scatter | solution.py:1050
  352.4 25.0 %collective-permute-start.46 = (bf16[256,1024]{1,0:T(8,128)(2,1)S(1)}, bf16[256,1024]{1,0:T(8,128)(2,1)S(1)}, u32[]{:S(2)}, u32[]{:S(2)}) collective-permute-start(bf16[256,1024]{1,0:T(8,128)(2,1)S(1)} %get-tuple-element.308), channel_id=1, source_target_pairs={{0,32},{32,64},{64,96},{96,0},{1,33},{33,65},{65,97},{97,1},{2,34}... | collective-permute-start | bytes 1572872 | tf_op jit(solution)/shard_map/ppermute | solution.py:46
  386.9 26.5 %collective-permute-start.48 = (bf16[256,1024]{1,0:T(8,128)(2,1)S(1)}, bf16[256,1024]{1,0:T(8,128)(2,1)S(1)}, u32[]{:S(2)}, u32[]{:S(2)}) collective-permute-start(bf16[256,1024]{1,0:T(8,128)(2,1)S(1)} %get-tuple-element.285), channel_id=1, source_target_pairs={{0,32},{32,64},{64,96},{96,0},{1,33},{33,65},{65,97},{97,1},{2,34}... | collective-permute-start | bytes 1572872 | tf_op jit(solution)/shard_map/ppermute | solution.py:46
  387.2 26.2 %collective-permute-start.49 = (bf16[256,1024]{1,0:T(8,128)(2,1)S(1)}, bf16[256,1024]{1,0:T(8,128)(2,1)S(1)}, u32[]{:S(2)}, u32[]{:S(2)}) collective-permute-start(bf16[256,1024]{1,0:T(8,128)(2,1)S(1)} %get-tuple-element.285), channel_id=1, source_target_pairs={{0,64},{32,96},{64,0},{96,32},{1,65},{33,97},{65,1},{97,33},{2,66}... | collective-permute-start | bytes 1572872 | tf_op jit(solution)/shard_map/ppermute | solution.py:46
  389.3 24.7 %collective-permute-start.50 = (bf16[256,1024]{1,0:T(8,128)(2,1)S(1)}, bf16[256,1024]{1,0:T(8,128)(2,1)S(1)}, u32[]{:S(2)}, u32[]{:S(2)}) collective-permute-start(bf16[256,1024]{1,0:T(8,128)(2,1)S(1)} %get-tuple-element.285), channel_id=1, source_target_pairs={{0,96},{32,0},{64,32},{96,64},{1,97},{33,1},{65,33},{97,65},{2,98}... | collective-permute-start | bytes 1572872 | tf_op jit(solution)/shard_map/ppermute | solution.py:46
  422.0 28.9 %collective-permute-start.56 = (bf16[256,1024]{1,0:T(8,128)(2,1)}, bf16[256,1024]{1,0:T(8,128)(2,1)}, u32[]{:S(2)}, u32[]{:S(2)}) collective-permute-start(bf16[256,1024]{1,0:T(8,128)(2,1)} %get-tuple-element.305), channel_id=1, source_target_pairs={{0,96},{32,0},{64,32},{96,64},{1,97},{33,1},{65,33},{97,65},{2,98}... | collective-permute-start | bytes 1572872 | tf_op jit(solution)/shard_map/ppermute | solution.py:46
  424.8 26.1 %collective-permute-start.57 = (bf16[256,1024]{1,0:T(8,128)(2,1)}, bf16[256,1024]{1,0:T(8,128)(2,1)}, u32[]{:S(2)}, u32[]{:S(2)}) collective-permute-start(bf16[256,1024]{1,0:T(8,128)(2,1)} %get-tuple-element.307), channel_id=1, source_target_pairs={{0,64},{32,96},{64,0},{96,32},{1,65},{33,97},{65,1},{97,33},{2,66}... | collective-permute-start | bytes 1572872 | tf_op jit(solution)/shard_map/ppermute | solution.py:46
  425.3 26.5 %collective-permute-start.58 = (bf16[256,1024]{1,0:T(8,128)(2,1)}, bf16[256,1024]{1,0:T(8,128)(2,1)}, u32[]{:S(2)}, u32[]{:S(2)}) collective-permute-start(bf16[256,1024]{1,0:T(8,128)(2,1)} %get-tuple-element.306), channel_id=1, source_target_pairs={{0,32},{32,64},{64,96},{96,0},{1,33},{33,65},{65,97},{97,1},{2,34}... | collective-permute-start | bytes 1572872 | tf_op jit(solution)/shard_map/ppermute | solution.py:46
  468.6 18.4 %collective-permute-start.59 = (bf16[1024,1024]{1,0:T(8,128)(2,1)}, bf16[1024,1024]{1,0:T(8,128)(2,1)}, u32[]{:S(2)}, u32[]{:S(2)}) collective-permute-start(bf16[1024,1024]{1,0:T(8,128)(2,1)} %get-tuple-element.211), channel_id=1, source_target_pairs={{0,1},{1,0},{2,3},{3,2},{4,5},{5,4},{6,7},{7,6},{8,9},{9,8},{10,11... | collective-permute-start | bytes 6291464 | tf_op jit(solution)/shard_map/ppermute | solution.py:42
  507.0 30.9 %collective-permute-start.60 = (bf16[4,64,1152]{2,1,0:T(8,128)(2,1)S(1)}, bf16[4,64,1152]{2,1,0:T(8,128)(2,1)S(1)}, u32[]{:S(2)}, u32[]{:S(2)}) collective-permute-start(bf16[4,64,1152]{2,1,0:T(8,128)(2,1)S(1)} %get-tuple-element.224), channel_id=1, source_target_pairs={{0,2},{2,4},{4,6},{6,0},{1,3},{3,5},{5,7},{7,1},{8,10},{10,12},{12... | collective-permute-start | bytes 1769480 | tf_op jit(solution)/shard_map/ppermute | solution.py:106
  509.9 26.8 %collective-permute-start.68 = (bf16[256,1024]{1,0:T(8,128)(2,1)S(1)}, bf16[256,1024]{1,0:T(8,128)(2,1)S(1)}, u32[]{:S(2)}, u32[]{:S(2)}) collective-permute-start(bf16[256,1024]{1,0:T(8,128)(2,1)S(1)} %copy-done.18), channel_id=1, source_target_pairs={{0,32},{32,64},{64,96},{96,0},{1,33},{33,65},{65,97},{97,1},{2,34}... | collective-permute-start | bytes 1572872 | tf_op jit(solution)/shard_map/ppermute | solution.py:46
  510.5 32.8 %collective-permute-start.61 = (bf16[4,64,1152]{2,1,0:T(8,128)(2,1)}, bf16[4,64,1152]{2,1,0:T(8,128)(2,1)S(1)}, u32[]{:S(2)}, u32[]{:S(2)}) collective-permute-start(bf16[4,64,1152]{2,1,0:T(8,128)(2,1)} %get-tuple-element.225), channel_id=1, source_target_pairs={{0,4},{2,6},{4,0},{6,2},{1,5},{3,7},{5,1},{7,3},{8,12},{10,14},{12... | collective-permute-start | bytes 1769480 | tf_op jit(solution)/shard_map/ppermute | solution.py:106
  523.2 20.1 %collective-permute-start.62 = (bf16[4,64,1152]{2,1,0:T(8,128)(2,1)}, bf16[4,64,1152]{2,1,0:T(8,128)(2,1)}, u32[]{:S(2)}, u32[]{:S(2)}) collective-permute-start(bf16[4,64,1152]{2,1,0:T(8,128)(2,1)} %get-tuple-element.226), channel_id=1, source_target_pairs={{0,6},{2,0},{4,2},{6,4},{1,7},{3,1},{5,3},{7,5},{8,14},{10,8},{12,... | collective-permute-start | bytes 1769480 | tf_op jit(solution)/shard_map/ppermute | solution.py:106
  536.7 17.8 %collective-permute-start.64 = (bf16[4,64,1152]{2,1,0:T(8,128)(2,1)S(1)}, bf16[4,64,1152]{2,1,0:T(8,128)(2,1)}, u32[]{:S(2)}, u32[]{:S(2)}) collective-permute-start(bf16[4,64,1152]{2,1,0:T(8,128)(2,1)S(1)} %get-tuple-element.229), channel_id=1, source_target_pairs={{0,16},{8,24},{16,0},{24,8},{1,17},{9,25},{17,1},{25,9},{2,18},{10... | collective-permute-start | bytes 1769480 | tf_op jit(solution)/shard_map/ppermute | solution.py:106
  538.0 28.0 %collective-permute-start.65 = (bf16[4,64,1152]{2,1,0:T(8,128)(2,1)S(1)}, bf16[4,64,1152]{2,1,0:T(8,128)(2,1)}, u32[]{:S(2)}, u32[]{:S(2)}) collective-permute-start(bf16[4,64,1152]{2,1,0:T(8,128)(2,1)S(1)} %get-tuple-element.230), channel_id=1, source_target_pairs={{0,24},{8,0},{16,8},{24,16},{1,25},{9,1},{17,9},{25,17},{2,26},{10... | collective-permute-start | bytes 1769480 | tf_op jit(solution)/shard_map/ppermute | solution.py:106
  588.3 21.8 %collective-permute-start.72 = (bf16[128,1024]{1,0:T(8,128)(2,1)S(1)}, bf16[128,1024]{1,0:T(8,128)(2,1)S(1)}, u32[]{:S(2)}, u32[]{:S(2)}) collective-permute-start(bf16[128,1024]{1,0:T(8,128)(2,1)S(1)} %broadcast_select_fusion.3), channel_id=1, source_target_pairs={{0,16},{16,0},{1,17},{17,1},{2,18},{18,2},{3,19},{19,3},{4,20},{20... | collective-permute-start | bytes 786440 | tf_op jit(solution)/shard_map/ppermute | solution.py:137
  599.1 18.2 %collective-permute-start.70 = (bf16[128,1024]{1,0:T(8,128)(2,1)S(1)}, bf16[128,1024]{1,0:T(8,128)(2,1)S(1)}, u32[]{:S(2)}, u32[]{:S(2)}) collective-permute-start(bf16[128,1024]{1,0:T(8,128)(2,1)S(1)} %get-tuple-element.283), channel_id=1, source_target_pairs={{0,1},{1,0},{2,3},{3,2},{4,5},{5,4},{6,7},{7,6},{8,9},{9,8},{10,11... | collective-permute-start | bytes 786440 | tf_op jit(solution)/shard_map/ppermute | solution.py:42
  (107 other events, 1223.3 us)
Sparse Core Ops, SparseCore 0:
  33.5 54.9 all-gather.5
  90.6 89.7 all-gather.7
  182.5 89.7 all-gather.9
  282.2 93.1 reduce-scatter.2
  378.7 93.4 reduce-scatter.4
